TPU v7x, 32 devices: a whole 2x2x4 slice. The times are simulated.
32 devices in a mesh: dp: 16 (over z, x, core), tensor: 2 (over y).
Axes of the slice: x: 2, y: 2, z: 4, core: 2. Of those that a mesh axis runs over, the one named last changes fastest.
Arguments:
- tokens: bfloat16 [8192, 3072], P('dp', 'tensor'), may hold values from -6 to 6
- hidden_cot: bfloat16 [8192, 8192], P('dp', 'tensor'), may hold values from -1.5 to 1.5
- w_gate: bfloat16 [3072, 8192], P(None, 'tensor'), may hold values from -0.109375 to 0.109375
- w_up: bfloat16 [3072, 8192], P(None, 'tensor'), may hold values from -0.109375 to 0.109375
- expert_ids: int32 [8192, 2], P('dp'), may hold values from 0 to 7, as said below
- route_fixed: int32 [8192, 2], P('dp'), may hold values from 4096 to 65535
Outputs:
- token_grad: bfloat16 [8192, 3072], P('dp', 'tensor')
- gate_grad: bfloat16 [3072, 8192], P('dp', 'tensor')
- up_grad: bfloat16 [3072, 8192], P('dp', 'tensor')
- route_grad: float32 [8192], P('dp')
Inputs may be any that keep to these rules, and one draw needn't show every extreme that they name: `expert_ids`: each row names 2 different experts; in each aligned block of 512 rows (the rows of one index of dp), between 128 and 256 rows name expert 0, and exactly 256 in some block.
All inputs are finite; a program needn't handle non-finite values.
Results may differ from a plain program's by a relative error of at most 0.0049.
Values may be sent and summed in bfloat16 or wider, within the bound.
A program may use at most 256 MiB of HBM per device.

v0:
```python
import jax
import jax.numpy as jnp
from jax import lax
from jax.sharding import PartitionSpec as P

CAP = 256


def on_device(tokens, hidden_cot, w_gate, w_up, expert_ids, route_fixed):
    selected = expert_ids == 0
    routed_flag = jnp.any(selected, axis=1)
    slot_of = jnp.cumsum(routed_flag.astype(jnp.int32)) - 1
    slot_ids = jnp.arange(CAP, dtype=jnp.int32)
    dispatch_mask = (slot_of[None, :] == slot_ids[:, None]) & routed_flag[None, :]
    dispatch = dispatch_mask.astype(jnp.bfloat16)
    dispatch_wide = dispatch_mask.astype(jnp.float32)
    share_all = jnp.sum(jnp.where(selected, route_fixed, 0), axis=1).astype(jnp.float32) / 65536.0
    share = jnp.dot(dispatch_wide, share_all, precision=lax.Precision.HIGHEST)
    routed = jnp.sum(dispatch_wide, axis=1)
    picked = jnp.dot(dispatch, tokens, preferred_element_type=jnp.float32).astype(jnp.bfloat16)
    cot_rows = jnp.dot(dispatch, hidden_cot, preferred_element_type=jnp.float32).astype(
        jnp.bfloat16
    )
    gathered = lax.all_gather(picked, "tensor", axis=1, tiled=True)
    gate_pre = jnp.dot(gathered, w_gate, preferred_element_type=jnp.float32)
    up_pre = jnp.dot(gathered, w_up, preferred_element_type=jnp.float32)
    sigmoid_gate = jax.nn.sigmoid(gate_pre)
    activated = gate_pre * sigmoid_gate
    hidden = (activated * up_pre).astype(jnp.bfloat16)
    hidden = lax.optimization_barrier(hidden)
    hidden_wide = hidden.astype(jnp.float32)
    cot_wide = cot_rows.astype(jnp.float32)
    slot_route = routed * lax.psum(jnp.sum(hidden_wide * cot_wide, axis=1), "tensor")
    route_grad = jnp.dot(slot_route, dispatch_wide, precision=lax.Precision.HIGHEST)
    scaled = share[:, None] * cot_wide
    gate_cot = (scaled * up_pre * sigmoid_gate * (1.0 + gate_pre * (1.0 - sigmoid_gate))).astype(
        jnp.bfloat16
    )
    up_cot = (scaled * activated).astype(jnp.bfloat16)
    hidden_width = w_gate.shape[1]
    dims = (((1,), (1,)), ((), ()))
    first = lax.dot_general(w_gate, gate_cot, dims, preferred_element_type=jnp.float32)
    transposed = lax.psum_scatter(
        first + lax.dot_general(w_up, up_cot, dims, preferred_element_type=jnp.float32),
        "tensor",
        scatter_dimension=0,
        tiled=True,
    )
    slot_grad = transposed.T.astype(jnp.bfloat16)
    back_dims = (((0,), (0,)), ((), ()))
    token_grad = lax.dot_general(
        dispatch, slot_grad, back_dims, preferred_element_type=jnp.float32
    ).astype(jnp.bfloat16)
    rows_dims = (((0,), (0,)), ((), ()))
    stacked_cot = jnp.concatenate([gate_cot, up_cot], axis=1)
    summed = lax.psum_scatter(
        lax.dot_general(gathered, stacked_cot, rows_dims, preferred_element_type=jnp.float32),
        "dp",
        scatter_dimension=0,
        tiled=True,
    )
    gate_grad = summed[:, :hidden_width]
    up_grad = summed[:, hidden_width:]
    return (token_grad, gate_grad.astype(jnp.bfloat16), up_grad.astype(jnp.bfloat16), route_grad)


def solution(mesh):
    return jax.shard_map(
        on_device,
        mesh=mesh,
        in_specs=(
            P("dp", "tensor"),
            P("dp", "tensor"),
            P(None, "tensor"),
            P(None, "tensor"),
            P("dp", None),
            P("dp", None),
        ),
        out_specs=(P("dp", "tensor"), P("dp", "tensor"), P("dp", "tensor"), P("dp")),
        check_vma=False,
    )
```

profile of v0, /device:TPU:0, one launch (start us, length us, event | category | flops | bytes accessed | tf_op | source)
XLA Modules:
  0.0 1065.0 jit_solution(3307292840991210187)
XLA Ops:
  7.2 0.0 copy-start
  7.2 0.0 copy-start.4
  7.2 0.0 copy-start.5
  7.2 0.0 all-gather.2.cloned.1.call-start
  7.2 0.8 fusion.32
  8.1 0.3 reduce-window.9
  8.4 0.1 slice.15
  8.5 0.1 slice_reduce_fusion
  8.6 0.1 add_bitcast_fusion
  8.7 0.0 copy-done
  8.7 1.5 convolution_convert_fusion.2
  10.1 0.0 all-gather.2.cloned.1.call-update
  10.2 0.0 reduce-scatter.3.cloned.1.call-start
  10.3 0.3 fusion.20
  10.6 4.8 convolution_convert_fusion
  15.4 24.8 %all-gather.2.cloned.1.call-done = bf16[256,3072]{1,0:T(8,128)(2,1)} async-done(((bf16[256,1536]{1,0:T(8,128)(2,1)}), bf16[256,3072]{1,0:T(8,128)(2,1)}) %all-gather.2.cloned.1.call-update) | async-done | bytes 1572880 | tf_op jit(solution)/shard_map/all_gather | solution.py:24
  40.2 12.2 %fusion.35 = f32[256,4096]{1,0:T(8,128)S(1)} fusion(bf16[256,3072]{1,0:T(8,128)(2,1)} %all-gather.2.cloned.1.call-done, bf16[3072,4096]{1,0:T(8,128)(2,1)} %param.8), kind=kOutput, calls=%fused_computation.46 | convolution fusion | flops 6442450944 | bytes 30932992 | tf_op jit(solution)/shard_map/dot_general | solution.py:25
  52.4 14.8 %multiply_convert_fusion = (bf16[256,4096]{1,0:T(8,128)(2,1)}, bf16[256,4096]{1,0:T(8,128)(2,1)}, bf16[256,4096]{1,0:T(8,128)(2,1)}) fusion(f32[256,4096]{1,0:T(8,128)S(1)} %fusion.35, bf16[256,4096]{1,0:T(8,128)(2,1)S(1)} %copy-done.2, f32[256]{0:T(256)S(1)} %bitcast.26, bf16[256,3072]{1,0:T(8,128)(2,1)S(1)} %copy-done.3, bf16[3072,4096]{1,0:T(8,128)(2,1)} %param.9), kind=kOutput, calls=%fused_computation.14 | convolution fusion | flops 6460276736 | bytes 39322624 | tf_op jit(solution)/shard_map/dot_general | solution.py:26
  67.2 13.4 %fusion.36 = f32[256,3072]{1,0:T(8,128)} fusion(bf16[256,4096]{1,0:T(8,128)(2,1)} %get-tuple-element.5, bf16[3072,4096]{1,0:T(8,128)(2,1)} %param.8), kind=kOutput, calls=%fused_computation.47 | convolution fusion | flops 6442450944 | bytes 30408704 | tf_op jit(solution)/shard_map/dot_general | solution.py:42
  80.6 14.2 %fusion.12 = f32[3072,256]{0,1:T(8,128)} fusion(f32[256,3072]{1,0:T(8,128)} %fusion.36, bf16[256,4096]{1,0:T(8,128)(2,1)} %get-tuple-element.6, bf16[3072,4096]{1,0:T(8,128)(2,1)} %param.9), kind=kOutput, calls=%fused_computation.18 | convolution fusion | flops 6443237376 | bytes 33554432 | tf_op jit(solution)/shard_map/dot_general | solution.py:44
  94.8 0.0 reduce-scatter.3.cloned.1.call-update
  94.8 0.0 reduce-scatter.5.cloned.1.call-start
  94.9 37.8 %fusion.7 = f32[3072,8192]{1,0:T(8,128)} fusion(bf16[256,3072]{1,0:T(8,128)(2,1)S(1)} %copy-done.3, bf16[256,4096]{1,0:T(8,128)(2,1)} %get-tuple-element.6, bf16[256,4096]{1,0:T(8,128)(2,1)} %get-tuple-element.5), kind=kOutput, calls=%fused_computation.10 | convolution fusion | flops 12893290496 | bytes 106430464 | tf_op jit(solution)/shard_map/dot_general | solution.py:57
  132.7 0.0 reduce-scatter.5.cloned.1.call-update
  132.7 0.2 convert_reduce_fusion
  132.9 2.9 fusion.6
  135.7 4.9 psum.7
  140.7 0.9 fusion.15
  141.6 3.2 convolution_convert_fusion.1
  144.7 908.6 %reduce-scatter.5.cloned.1.call-done = f32[192,8192]{1,0:T(8,128)} async-done(((f32[3072,8192]{1,0:T(8,128)}), f32[192,8192]{1,0:T(8,128)}) %reduce-scatter.5.cloned.1.call-update) | async-done | bytes 6291472 | tf_op jit(solution)/shard_map/reduce_scatter | solution.py:56
  1053.3 3.3 convert.5
  1056.6 1.9 fusion.34
  (14 shorter events, 0.1 us)
Async XLA Ops:
  7.2 1.5 copy-start
  7.2 3.0 copy-start.4
  7.2 3.0 copy-start.5
  7.2 33.0 %all-gather.2.cloned.1.call-start = ((), (), s32[]{:S(2)}) async-start(), calls=%async_computation.2 | async-start | bytes 2359296 | tf_op jit(solution)/shard_map/all_gather | solution.py:24
  10.2 131.4 %reduce-scatter.3.cloned.1.call-start = ((), (), s32[]{:S(2)}) async-start(), calls=%async_computation.3 | async-start | bytes 4718592 | tf_op jit(solution)/shard_map/reduce_scatter | solution.py:43
  40.2 12.2 %copy-start.2 = (bf16[256,4096]{1,0:T(8,128)(2,1)S(1)}, bf16[256,4096]{1,0:T(8,128)(2,1)}, u32[]{:S(2)}) copy-start(bf16[256,4096]{1,0:T(8,128)(2,1)} %convolution_convert_fusion) | copy-start | bytes 6291460
  40.2 12.2 %copy-start.3 = (bf16[256,3072]{1,0:T(8,128)(2,1)S(1)}, bf16[256,3072]{1,0:T(8,128)(2,1)}, u32[]{:S(2)}) copy-start(bf16[256,3072]{1,0:T(8,128)(2,1)} %all-gather.2.cloned.1.call-done) | copy-start | bytes 4718596
  94.8 958.5 %reduce-scatter.5.cloned.1.call-start = ((), (), s32[]{:S(2)}) async-start(), calls=%async_computation.4 | async-start | bytes 106954752 | tf_op jit(solution)/shard_map/reduce_scatter | solution.py:56
  1053.3 5.2 copy-start.1
Sparse Core Ops, SparseCore 0:
  10.3 29.9 all-gather.1
  95.0 43.3 reduce-scatter.2
  143.1 910.0 reduce-scatter.4
where the time goes:
time: 1070 us
  waiting for transfers between devices  933 us (87%)
  matrix products  103 us (10%)
  between operations  13.8 us (1%)
    reduce_scatter x1, waiting for transfers between devices, on_device(): lax.psum_scatter(lax.dot_general(gathered, stacked_cot, rows_dims, prefer...  909 us
    dot_general x1, matrix products, on_device(): lax.dot_general(gathered, stacked_cot, rows_dims, preferred_element_type=...  37.8 us
    all_gather x1, waiting for transfers between devices, on_device(): gathered = lax.all_gather(picked, 'tensor', axis=1, tiled=True)  24.8 us
  transfers between devices with their start and end apart: 3, of which 2 were waited for; matrix products, arithmetic and copies ran while one was open for 5% of the time, Pallas kernels for 0%

commit v1 on v0

v1 whole, which is shorter than its diff:
```python
import functools

import jax
import jax.numpy as jnp
from jax import lax
from jax.sharding import PartitionSpec as P

CAP = 256
CHUNKS = 4


def on_device(ndp, ntp, tokens, hidden_cot, w_gate, w_up, expert_ids, route_fixed):
    n_high = ndp // 8
    me = lax.axis_index("dp")
    core, x_at, z_low, z_high = me % 2, (me // 2) % 2, (me // 4) % 2, me // 8
    tensor_at = lax.axis_index("tensor")
    is_gate = core == 0

    def flip(value, bit):
        return lax.ppermute(value, "dp", [(i, i ^ bit) for i in range(ndp)])

    def shift_high(value, step):
        return lax.ppermute(value, "dp", [(i, (i + 8 * step) % ndp) for i in range(ndp)])

    def shift_tensor(value, step):
        return lax.ppermute(value, "tensor", [(i, (i + step) % ntp) for i in range(ntp)])

    selected = expert_ids == 0
    routed_flag = jnp.any(selected, axis=1)
    slot_of = jnp.cumsum(routed_flag.astype(jnp.int32)) - 1
    slot_ids = jnp.arange(CAP, dtype=jnp.int32)
    dispatch_mask = (slot_of[None, :] == slot_ids[:, None]) & routed_flag[None, :]
    dispatch = dispatch_mask.astype(jnp.bfloat16)
    dispatch_wide = dispatch_mask.astype(jnp.float32)
    share_all = jnp.sum(jnp.where(selected, route_fixed, 0), axis=1).astype(jnp.float32) / 65536.0
    share = jnp.dot(dispatch_wide, share_all, precision=lax.Precision.HIGHEST)
    routed = jnp.sum(dispatch_wide, axis=1)
    picked = jnp.dot(dispatch, tokens, preferred_element_type=jnp.float32).astype(jnp.bfloat16)
    gathered = lax.all_gather(picked, "tensor", axis=1, tiled=True)
    cot_rows = jnp.dot(dispatch, hidden_cot, preferred_element_type=jnp.float32).astype(
        jnp.bfloat16
    )

    depth = gathered.shape[1] // ndp
    features = gathered.reshape(CAP, n_high, 2, 2, 2 * depth)
    near = lax.dynamic_index_in_dim(features, z_low, 2, keepdims=False)
    far = flip(lax.dynamic_index_in_dim(features, 1 - z_low, 2, keepdims=False), 4)
    both = jnp.stack([near, far])
    here = lax.dynamic_index_in_dim(both, x_at, 3, keepdims=False)
    there = flip(lax.dynamic_index_in_dim(both, 1 - x_at, 3, keepdims=False), 2)
    mine = jnp.concatenate([here, there])
    group = jnp.stack([mine, flip(mine, 1)], axis=1)
    group = group.reshape(8 * CAP, n_high, 2 * depth)
    group_of = [
        lax.dynamic_index_in_dim(group, (z_high + s) % n_high, 1, keepdims=False)
        for s in range(n_high)
    ]

    width = w_gate.shape[1]
    step = width // CHUNKS
    route_sum = jnp.zeros((CAP,), jnp.float32)
    gate_cots, up_cots, gates, ups = [], [], [], []
    rows_dims = (((0,), (0,)), ((), ()))
    for chunk in range(CHUNKS):
        columns = slice(chunk * step, (chunk + 1) * step)
        gate_pre = jnp.dot(gathered, w_gate[:, columns], preferred_element_type=jnp.float32)
        up_pre = jnp.dot(gathered, w_up[:, columns], preferred_element_type=jnp.float32)
        sigmoid_gate = jax.nn.sigmoid(gate_pre)
        activated = gate_pre * sigmoid_gate
        hidden = (activated * up_pre).astype(jnp.bfloat16)
        hidden = lax.optimization_barrier(hidden)
        cot_wide = cot_rows[:, columns].astype(jnp.float32)
        route_sum += jnp.sum(hidden.astype(jnp.float32) * cot_wide, axis=1)
        scaled = share[:, None] * cot_wide
        gate_cot = (
            scaled * up_pre * sigmoid_gate * (1.0 + gate_pre * (1.0 - sigmoid_gate))
        ).astype(jnp.bfloat16)
        up_cot = (scaled * activated).astype(jnp.bfloat16)
        gate_cots.append(gate_cot)
        up_cots.append(up_cot)
        kept = jnp.where(is_gate, gate_cot, up_cot)
        pair = jnp.concatenate([kept, flip(jnp.where(is_gate, up_cot, gate_cot), 1)])
        z_pair = flip(pair, 4)
        x_pair = flip(pair, 2)
        xz_pair = flip(z_pair, 2)
        cots = jnp.concatenate([pair, z_pair, x_pair, xz_pair])
        arrived = []
        for s in range(1, n_high):
            partial = lax.dot_general(
                group_of[s], cots, rows_dims, preferred_element_type=jnp.float32
            ).astype(jnp.bfloat16)
            arrived.append(shift_high(partial, s))
        total = lax.dot_general(group_of[0], cots, rows_dims, preferred_element_type=jnp.float32)
        for term in arrived:
            total += term.astype(jnp.float32)
        total = total.astype(jnp.bfloat16).reshape(2, depth, step)
        own = lax.dynamic_index_in_dim(total, core, 0, keepdims=False)
        other = flip(lax.dynamic_index_in_dim(total, 1 - core, 0, keepdims=False), 1)
        gates.append(jnp.where(is_gate, own, other))
        ups.append(jnp.where(is_gate, other, own))
    gate_grad = jnp.concatenate(gates, axis=1)
    up_grad = jnp.concatenate(ups, axis=1)

    slot_route = route_sum
    for s in range(1, ntp):
        slot_route += shift_tensor(route_sum, s)
    route_grad = jnp.dot(routed * slot_route, dispatch_wide, precision=lax.Precision.HIGHEST)

    dims = (((1,), (1,)), ((), ()))
    transposed = lax.dot_general(
        w_gate, jnp.concatenate(gate_cots, axis=1), dims, preferred_element_type=jnp.float32
    )
    transposed += lax.dot_general(
        w_up, jnp.concatenate(up_cots, axis=1), dims, preferred_element_type=jnp.float32
    )
    blocks = transposed.reshape(ntp, -1, CAP)
    slot_grad = lax.dynamic_index_in_dim(blocks, tensor_at, 0, keepdims=False)
    for s in range(1, ntp):
        to = lax.dynamic_index_in_dim(blocks, (tensor_at + s) % ntp, 0, keepdims=False)
        slot_grad += shift_tensor(to, s)
    back_dims = (((0,), (0,)), ((), ()))
    token_grad = lax.dot_general(
        dispatch,
        slot_grad.T.astype(jnp.bfloat16),
        back_dims,
        preferred_element_type=jnp.float32,
    ).astype(jnp.bfloat16)
    return token_grad, gate_grad, up_grad, route_grad


def solution(mesh):
    return jax.shard_map(
        functools.partial(on_device, mesh.shape["dp"], mesh.shape["tensor"]),
        mesh=mesh,
        in_specs=(
            P("dp", "tensor"),
            P("dp", "tensor"),
            P(None, "tensor"),
            P(None, "tensor"),
            P("dp", None),
            P("dp", None),
        ),
        out_specs=(P("dp", "tensor"), P("dp", "tensor"), P("dp", "tensor"), P("dp")),
        check_vma=False,
    )
```

time: 1070 us -> 496 us (0.46)
  waiting for transfers between devices: 933 us -> 322 us
  starting transfers between devices: 0.12 us -> 23.3 us
  local copies, waits for them, and re-layouts: 2.09 us -> 19.6 us
    reduce_scatter x2 -> x0, waiting for transfers between devices: 909 us -> none  [the longest x1 909 us: on_device(): lax.psum_scatter(lax.dot_general(gathered, stacked_cot, rows_dims, prefer...]
    ppermute x0 -> x29, waiting for transfers between devices: none -> 296 us  [the longest x23 175 us: flip(): return lax.ppermute(value, 'dp', [(i, i ^ bit) for i in range(ndp)])]
    ppermute x0 -> x29, starting transfers between devices: none -> 23.3 us  [the longest x23 16.2 us: flip(): return lax.ppermute(value, 'dp', [(i, i ^ bit) for i in range(ndp)])]
    dot_general x7 -> x20, matrix products: 96.4 us -> 88.4 us  [the longest x4 22.4 us: on_device(): jnp.dot(gathered, w_gate[:, columns], preferred_element_type=jnp.float32)]
  transfers between devices with their start and end apart: 3 -> 30, of which waited for: 2 -> 17; matrix products, arithmetic and copies ran while one was open for 5% -> 15% of each run, Pallas kernels for 0% -> 0%
where the time goes in v1:
time: 496 us; the launch traced here: 487 us
  waiting for transfers between devices  322 us (65%)
  matrix products  93.7 us (19%)
  starting transfers between devices  23.3 us (5%)
  local copies, waits for them, and re-layouts  19.6 us (4%)
  between operations  15.2 us (3%)
  other arithmetic  13.6 us (3%)
    ppermute x23, waiting for transfers between devices, flip(): return lax.ppermute(value, 'dp', [(i, i ^ bit) for i in range(ndp)])  175 us
    ppermute x4, waiting for transfers between devices, shift_high(): lax.ppermute(value, 'dp', [(i, (i + 8 * step) % ndp) for i in range(ndp)])  118 us
    all_gather x1, waiting for transfers between devices, on_device(): gathered = lax.all_gather(picked, 'tensor', axis=1, tiled=True)  25.9 us
    dot_general x4, matrix products, on_device(): jnp.dot(gathered, w_gate[:, columns], preferred_element_type=jnp.float32)  22.4 us
    dot_general x4, matrix products, on_device(): jnp.dot(gathered, w_up[:, columns], preferred_element_type=jnp.float32)  21.6 us
    ppermute x23, starting transfers between devices, flip(): return lax.ppermute(value, 'dp', [(i, i ^ bit) for i in range(ndp)])  16.2 us
    dot_general x1, matrix products, on_device(): lax.dot_general(w_up, jnp.concatenate(up_cots, axis=1), dims, preferred_e...  13.9 us
    dot_general x1, matrix products, on_device(): lax.dot_general(w_gate, jnp.concatenate(gate_cots, axis=1), dims, preferr...  13 us
  transfers between devices with their start and end apart: 30, of which 17 were waited for; matrix products, arithmetic and copies ran while one was open for 15% of the time, Pallas kernels for 0%

profile of v1, /device:TPU:0, one launch (start us, length us, event | category | flops | bytes accessed | tf_op | source)
XLA Modules:
  0.0 486.8 jit_solution(5223523124783631077)
XLA Ops:
  10.9 3.5 convolution_convert_fusion
  14.3 25.9 %all-gather.2.cloned.1.call-done = bf16[256,3072]{1,0:T(8,128)(2,1)} async-done(((bf16[256,1536]{1,0:T(8,128)(2,1)}), bf16[256,3072]{1,0:T(8,128)(2,1)}) %all-gather.2.cloned.1.call-update) | async-done | bytes 1572880 | tf_op jit(solution)/shard_map/all_gather | solution.py:39
  40.2 5.2 %fusion.8 = f32[256,1024]{1,0:T(8,128)S(1)} fusion(bf16[256,3072]{1,0:T(8,128)(2,1)} %all-gather.2.cloned.1.call-done, bf16[3072,4096]{1,0:T(8,128)(2,1)} %param.8), kind=kOutput, calls=%fused_computation.8 | convolution fusion | flops 1610612736 | bytes 8912896 | tf_op jit(solution)/shard_map/dot_general | solution.py:66
  45.4 4.6 fusion.4
  50.0 4.6 fusion
  54.7 4.6 fusion.14
  59.3 5.5 %multiply_convert_fusion.2 = (bf16[256,1024]{1,0:T(8,128)(2,1)}, f32[256,1024]{1,0:T(8,128)S(1)}) fusion(f32[256,1024]{1,0:T(8,128)S(1)} %fusion.8, bf16[256,3072]{1,0:T(8,128)(2,1)S(1)} %copy-done.7, bf16[3072,4096]{1,0:T(8,128)(2,1)} %param.9), kind=kOutput, calls=%fused_computation.113 | convolution fusion | flops 1612185600 | bytes 10485760 | tf_op jit(solution)/shard_map/dot_general | solution.py:67
  64.8 5.5 %multiply_convert_fusion.1 = (bf16[256,1024]{1,0:T(8,128)(2,1)}, f32[256,1024]{1,0:T(8,128)S(1)}) fusion(f32[256,1024]{1,0:T(8,128)S(1)} %fusion.4, bf16[256,3072]{1,0:T(8,128)(2,1)S(1)} %copy-done.7, bf16[3072,4096]{1,0:T(8,128)(2,1)} %param.9), kind=kOutput, calls=%fused_computation.112 | convolution fusion | flops 1612185600 | bytes 10485760 | tf_op jit(solution)/shard_map/dot_general | solution.py:67
  70.4 5.9 %multiply_convert_fusion = (bf16[256,1024]{1,0:T(8,128)(2,1)}, f32[256,1024]{1,0:T(8,128)S(1)}) fusion(f32[256,1024]{1,0:T(8,128)S(1)} %fusion, bf16[256,3072]{1,0:T(8,128)(2,1)S(1)} %copy-done.7, bf16[3072,4096]{1,0:T(8,128)(2,1)} %param.9), kind=kOutput, calls=%fused_computation.111 | convolution fusion | flops 1612185600 | bytes 10485760 | tf_op jit(solution)/shard_map/dot_general | solution.py:67
  76.3 8.1 %broadcast_select_fusion.6 = (bf16[256,1024]{1,0:T(8,128)(2,1)}, bf16[256,1024]{1,0:T(8,128)(2,1)}, bf16[256,1024]{1,0:T(8,128)(2,1)}, bf16[256,1024]{1,0:T(8,12...) fusion(pred[]{:T(512)S(6)} %eq.34, ...), kind=kOutput, calls=%fused_computation.148 | convolution fusion | flops 1627389952 | bytes 24642560 | tf_op jit(solution)/shard_map/dot_general | solution.py:66
  87.2 2.0 constant_dynamic-slice_fusion
  93.4 13.0 %fusion.17 = f32[256,3072]{1,0:T(8,128)} fusion(bf16[3072,4096]{1,0:T(8,128)(2,1)} %param.8, bf16[256,1024]{1,0:T(8,128)(2,1)S(1)} %copy-done.9, bf16[256,1024]{1,0:T(8,128)(2,1)S(1)} %copy-done.14, bf16[256,1024]{1,0:T(8,128)(2,1)S(1)} %copy-done.20, bf16[256,1024]{1,0:T(8,128)(2,1)} %get-tuple-element.10), kind=kOutput, calls=%fused_computation.22 | convolution fusion | flops 6450839552 | bytes 30408704 | tf_op jit(solution)/shard_map/dot_general | solution.py:110
  106.5 13.9 %fusion.16 = f32[3072,256]{0,1:T(8,128)} fusion(f32[256,3072]{1,0:T(8,128)} %fusion.17, bf16[3072,4096]{1,0:T(8,128)(2,1)} %param.9, bf16[256,1024]{1,0:T(8,128)(2,1)S(1)} %copy-done.11, bf16[256,1024]{1,0:T(8,128)(2,1)S(1)} %copy-done.16, bf16[256,1024]{1,0:T(8,128)(2,1)S(1)} %copy-done.22, bf16[256,1024]{1,0:T(8,128)(2,1)} %get-tuple-element.9), kind=kOutput, calls=%fused_computation.18 | convolution fusion | flops 6451625984 | bytes 33554432 | tf_op jit(solution)/shard_map/dot_general | solution.py:113
  120.4 4.4 reshape.60
  124.9 2.7 constant_dynamic-slice_fusion.3
  133.6 2.0 collective-permute-done.28
  141.9 15.2 %collective-permute-done.5 = bf16[512,1024]{1,0:T(8,128)(2,1)S(1)} collective-permute-done((bf16[512,1024]{1,0:T(8,128)(2,1)S(1)}, bf16[512,1024]{1,0:T(8,128)(2,1)S(1)}, u32[]{:S(2)}, u32[]{:S(2)}) %collective-permute-start.5) | collective-permute-done | bytes 1048608 | tf_op jit(solution)/shard_map/ppermute | solution.py:20
  163.1 16.4 %collective-permute-done.11 = bf16[512,1024]{1,0:T(8,128)(2,1)S(1)} collective-permute-done((bf16[512,1024]{1,0:T(8,128)(2,1)S(1)}, bf16[512,1024]{1,0:T(8,128)(2,1)S(1)}, u32[]{:S(2)}, u32[]{:S(2)}) %collective-permute-start.11) | collective-permute-done | bytes 1048608 | tf_op jit(solution)/shard_map/ppermute | solution.py:20
  181.4 2.7 collective-permute-done.12
  185.6 16.4 %collective-permute-done.17 = bf16[512,1024]{1,0:T(8,128)(2,1)S(1)} collective-permute-done((bf16[512,1024]{1,0:T(8,128)(2,1)S(1)}, bf16[512,1024]{1,0:T(8,128)(2,1)S(1)}, u32[]{:S(2)}, u32[]{:S(2)}) %collective-permute-start.17) | collective-permute-done | bytes 1048608 | tf_op jit(solution)/shard_map/ppermute | solution.py:20
  207.0 37.3 %collective-permute-done.2 = bf16[2,256,2,384]{3,1,2,0:T(8,128)(2,1)S(1)} collective-permute-done((bf16[2,256,2,384]{3,1,2,0:T(8,128)(2,1)S(1)}, bf16[2,256,2,384]{3,1,2,0:T(8,128)(2,1)S(1)}, u32[]{:S(2)}, u32[]{:S(2)}) %collective-permute-start.2) | collective-permute-done | bytes 786464 | tf_op jit(solution)/shard_map/ppermute | solution.py:20
  251.0 19.4 %collective-permute-done.7 = bf16[512,1024]{1,0:T(8,128)(2,1)S(1)} collective-permute-done((bf16[512,1024]{1,0:T(8,128)(2,1)S(1)}, bf16[512,1024]{1,0:T(8,128)(2,1)S(1)}, u32[]{:S(2)}, u32[]{:S(2)}) %collective-permute-start.7) | collective-permute-done | bytes 1048608 | tf_op jit(solution)/shard_map/ppermute | solution.py:20
  270.4 22.4 %collective-permute-done.13 = bf16[512,1024]{1,0:T(8,128)(2,1)S(1)} collective-permute-done((bf16[512,1024]{1,0:T(8,128)(2,1)S(1)}, bf16[512,1024]{1,0:T(8,128)(2,1)S(1)}, u32[]{:S(2)}, u32[]{:S(2)}) %collective-permute-start.13) | collective-permute-done | bytes 1048608 | tf_op jit(solution)/shard_map/ppermute | solution.py:20
  292.9 22.4 %collective-permute-done.19 = bf16[512,1024]{1,0:T(8,128)(2,1)S(1)} collective-permute-done((bf16[512,1024]{1,0:T(8,128)(2,1)S(1)}, bf16[512,1024]{1,0:T(8,128)(2,1)S(1)}, u32[]{:S(2)}, u32[]{:S(2)}) %collective-permute-start.19) | collective-permute-done | bytes 1048608 | tf_op jit(solution)/shard_map/ppermute | solution.py:20
  315.4 19.8 %collective-permute-done.25 = bf16[512,1024]{1,0:T(8,128)(2,1)S(1)} collective-permute-done((bf16[512,1024]{1,0:T(8,128)(2,1)S(1)}, bf16[512,1024]{1,0:T(8,128)(2,1)S(1)}, u32[]{:S(2)}, u32[]{:S(2)}) %collective-permute-start.25) | collective-permute-done | bytes 1048608 | tf_op jit(solution)/shard_map/ppermute | solution.py:20
  337.9 2.5 collective-permute-start.8
  342.8 2.0 fusion.63
  344.8 2.5 collective-permute-start.20
  349.7 74.6 %collective-permute-done.8 = bf16[384,1024]{1,0:T(8,128)(2,1)S(1)} collective-permute-done((bf16[384,1024]{1,0:T(8,128)(2,1)S(1)}, bf16[384,1024]{1,0:T(8,128)(2,1)S(1)}, u32[]{:S(2)}, u32[]{:S(2)}) %collective-permute-start.8) | collective-permute-done | bytes 786464 | tf_op jit(solution)/shard_map/ppermute | solution.py:23
  426.3 14.9 %collective-permute-done.14 = bf16[384,1024]{1,0:T(8,128)(2,1)S(1)} collective-permute-done((bf16[384,1024]{1,0:T(8,128)(2,1)S(1)}, bf16[384,1024]{1,0:T(8,128)(2,1)S(1)}, u32[]{:S(2)}, u32[]{:S(2)}) %collective-permute-start.14) | collective-permute-done | bytes 786464 | tf_op jit(solution)/shard_map/ppermute | solution.py:23
  443.1 14.9 %collective-permute-done.20 = bf16[384,1024]{1,0:T(8,128)(2,1)S(1)} collective-permute-done((bf16[384,1024]{1,0:T(8,128)(2,1)S(1)}, bf16[384,1024]{1,0:T(8,128)(2,1)S(1)}, u32[]{:S(2)}, u32[]{:S(2)}) %collective-permute-start.20) | collective-permute-done | bytes 786464 | tf_op jit(solution)/shard_map/ppermute | solution.py:23
  460.0 13.8 %collective-permute-done.26 = bf16[384,1024]{1,0:T(8,128)(2,1)S(1)} collective-permute-done((bf16[384,1024]{1,0:T(8,128)(2,1)S(1)}, bf16[384,1024]{1,0:T(8,128)(2,1)S(1)}, u32[]{:S(2)}, u32[]{:S(2)}) %collective-permute-start.26) | collective-permute-done | bytes 786464 | tf_op jit(solution)/shard_map/ppermute | solution.py:23
  (168 shorter events, 62.9 us)
Async XLA Ops:
  7.2 33.0 %all-gather.2.cloned.1.call-start = ((), (), s32[]{:S(2)}) async-start(), calls=%async_computation | async-start | bytes 2359296 | tf_op jit(solution)/shard_map/all_gather | solution.py:39
  14.3 61.9 %copy-start.4 = (bf16[256,4096]{1,0:T(8,128)(2,1)}, bf16[256,4096]{1,0:T(8,128)(2,1)S(1)}, u32[]{:S(2)}) copy-start(bf16[256,4096]{1,0:T(8,128)(2,1)S(1)} %convolution_convert_fusion) | copy-start | bytes 6291460
  85.4 43.9 %collective-permute-start.4 = (bf16[256,1024]{1,0:T(8,128)(2,1)}, bf16[256,1024]{1,0:T(8,128)(2,1)}, u32[]{:S(2)}, u32[]{:S(2)}) collective-permute-start(bf16[256,1024]{1,0:T(8,128)(2,1)} %get-tuple-element.8), channel_id=1, source_target_pairs={{0,2},{2,0},{4,6},{6,4},{8,10},{10,8},{12,14},{14,12},{16,18},{18,... | collective-permute-start | bytes 1572872 | tf_op jit(solution)/shard_map/ppermute | solution.py:20
  90.1 50.2 %collective-permute-start.1 = (bf16[256,2,2,384]{3,0,2,1:T(8,128)(2,1)}, bf16[256,2,2,384]{3,0,2,1:T(8,128)(2,1)}, u32[]{:S(2)}, u32[]{:S(2)}) collective-permute-start(bf16[256,2,2,384]{3,0,2,1:T(8,128)(2,1)} %bitcast.113), channel_id=1, source_target_pairs={{0,8},{2,10},{4,12},{6,14},{8,0},{10,2},{12,4},{14,6},{16,24},{18,... | collective-permute-start | bytes 2359304 | tf_op jit(solution)/shard_map/ppermute | solution.py:20
  91.6 40.3 %collective-permute-start.10 = (bf16[256,1024]{1,0:T(8,128)(2,1)}, bf16[256,1024]{1,0:T(8,128)(2,1)}, u32[]{:S(2)}, u32[]{:S(2)}) collective-permute-start(bf16[256,1024]{1,0:T(8,128)(2,1)} %get-tuple-element.30), channel_id=1, source_target_pairs={{0,2},{2,0},{4,6},{6,4},{8,10},{10,8},{12,14},{14,12},{16,18},{18,... | collective-permute-start | bytes 1572872 | tf_op jit(solution)/shard_map/ppermute | solution.py:20
  91.6 45.5 %collective-permute-start.16 = (bf16[256,1024]{1,0:T(8,128)(2,1)}, bf16[256,1024]{1,0:T(8,128)(2,1)}, u32[]{:S(2)}, u32[]{:S(2)}) collective-permute-start(bf16[256,1024]{1,0:T(8,128)(2,1)} %get-tuple-element.33), channel_id=1, source_target_pairs={{0,2},{2,0},{4,6},{6,4},{8,10},{10,8},{12,14},{14,12},{16,18},{18,... | collective-permute-start | bytes 1572872 | tf_op jit(solution)/shard_map/ppermute | solution.py:20
  92.1 47.5 %collective-permute-start.22 = (bf16[256,1024]{1,0:T(8,128)(2,1)}, bf16[256,1024]{1,0:T(8,128)(2,1)}, u32[]{:S(2)}, u32[]{:S(2)}) collective-permute-start(bf16[256,1024]{1,0:T(8,128)(2,1)} %get-tuple-element.36), channel_id=1, source_target_pairs={{0,2},{2,0},{4,6},{6,4},{8,10},{10,8},{12,14},{14,12},{16,18},{18,... | collective-permute-start | bytes 1572872 | tf_op jit(solution)/shard_map/ppermute | solution.py:20
  131.1 26.0 %collective-permute-start.5 = (bf16[512,1024]{1,0:T(8,128)(2,1)S(1)}, bf16[512,1024]{1,0:T(8,128)(2,1)S(1)}, u32[]{:S(2)}, u32[]{:S(2)}) collective-permute-start(bf16[512,1024]{1,0:T(8,128)(2,1)S(1)} %pad_maximum_fusion.4), channel_id=1, source_target_pairs={{0,8},{2,10},{4,12},{6,14},{8,0},{10,2},{12,4},{14,6},{16,24},{18,... | collective-permute-start | bytes 3145736 | tf_op jit(solution)/shard_map/ppermute | solution.py:20
  131.9 3.6 collective-permute-start.28
  132.3 25.3 %copy-start.26 = (bf16[2048,1024]{1,0:T(8,128)(2,1)S(1)}, bf16[2048,1024]{1,0:T(8,128)(2,1)}, u32[]{:S(2)}) copy-start(bf16[2048,1024]{1,0:T(8,128)(2,1)} %get-tuple-element.11) | copy-start | bytes 12582916
  135.6 26.1 %collective-permute-start.6 = (bf16[512,1024]{1,0:T(8,128)(2,1)S(1)}, bf16[512,1024]{1,0:T(8,128)(2,1)S(1)}, u32[]{:S(2)}, u32[]{:S(2)}) collective-permute-start(bf16[512,1024]{1,0:T(8,128)(2,1)S(1)} %pad_maximum_fusion.4), channel_id=1, source_target_pairs={{0,4},{2,6},{4,0},{6,2},{8,12},{10,14},{12,8},{14,10},{16,20},{18,... | collective-permute-start | bytes 3145736 | tf_op jit(solution)/shard_map/ppermute | solution.py:20
  137.0 42.5 %collective-permute-start.11 = (bf16[512,1024]{1,0:T(8,128)(2,1)S(1)}, bf16[512,1024]{1,0:T(8,128)(2,1)S(1)}, u32[]{:S(2)}, u32[]{:S(2)}) collective-permute-start(bf16[512,1024]{1,0:T(8,128)(2,1)S(1)} %pad_maximum_fusion.5), channel_id=1, source_target_pairs={{0,8},{2,10},{4,12},{6,14},{8,0},{10,2},{12,4},{14,6},{16,24},{18,... | collective-permute-start | bytes 3145736 | tf_op jit(solution)/shard_map/ppermute | solution.py:20
  139.7 44.5 %collective-permute-start.12 = (bf16[512,1024]{1,0:T(8,128)(2,1)S(1)}, bf16[512,1024]{1,0:T(8,128)(2,1)S(1)}, u32[]{:S(2)}, u32[]{:S(2)}) collective-permute-start(bf16[512,1024]{1,0:T(8,128)(2,1)S(1)} %pad_maximum_fusion.5), channel_id=1, source_target_pairs={{0,4},{2,6},{4,0},{6,2},{8,12},{10,14},{12,8},{14,10},{16,20},{18,... | collective-permute-start | bytes 3145736 | tf_op jit(solution)/shard_map/ppermute | solution.py:20
  140.3 61.8 %collective-permute-start.17 = (bf16[512,1024]{1,0:T(8,128)(2,1)S(1)}, bf16[512,1024]{1,0:T(8,128)(2,1)S(1)}, u32[]{:S(2)}, u32[]{:S(2)}) collective-permute-start(bf16[512,1024]{1,0:T(8,128)(2,1)S(1)} %pad_maximum_fusion.6), channel_id=1, source_target_pairs={{0,8},{2,10},{4,12},{6,14},{8,0},{10,2},{12,4},{14,6},{16,24},{18,... | collective-permute-start | bytes 3145736 | tf_op jit(solution)/shard_map/ppermute | solution.py:20
  157.1 91.3 %collective-permute-start = (f32[1536,256]{0,1:T(8,128)S(1)}, f32[1536,256]{0,1:T(8,128)S(1)}, u32[]{:S(2)}, u32[]{:S(2)}) collective-permute-start(f32[1536,256]{0,1:T(8,128)S(1)} %bitcast.124), channel_id=1, source_target_pairs={{0,1},{1,0},{2,3},{3,2},{4,5},{5,4},{6,7},{7,6},{8,9},{9,8},{10,11... | collective-permute-start | bytes 4718600 | tf_op jit(solution)/shard_map/ppermute | solution.py:26
  161.7 84.4 %collective-permute-start.18 = (bf16[512,1024]{1,0:T(8,128)(2,1)S(1)}, bf16[512,1024]{1,0:T(8,128)(2,1)S(1)}, u32[]{:S(2)}, u32[]{:S(2)}) collective-permute-start(bf16[512,1024]{1,0:T(8,128)(2,1)S(1)} %pad_maximum_fusion.6), channel_id=1, source_target_pairs={{0,4},{2,6},{4,0},{6,2},{8,12},{10,14},{12,8},{14,10},{16,20},{18,... | collective-permute-start | bytes 3145736 | tf_op jit(solution)/shard_map/ppermute | solution.py:20
  179.6 67.1 %collective-permute-start.23 = (bf16[512,1024]{1,0:T(8,128)(2,1)S(1)}, bf16[512,1024]{1,0:T(8,128)(2,1)S(1)}, u32[]{:S(2)}, u32[]{:S(2)}) collective-permute-start(bf16[512,1024]{1,0:T(8,128)(2,1)S(1)} %pad_maximum_fusion.7), channel_id=1, source_target_pairs={{0,8},{2,10},{4,12},{6,14},{8,0},{10,2},{12,4},{14,6},{16,24},{18,... | collective-permute-start | bytes 3145736 | tf_op jit(solution)/shard_map/ppermute | solution.py:20
  184.1 62.6 %collective-permute-start.24 = (bf16[512,1024]{1,0:T(8,128)(2,1)S(1)}, bf16[512,1024]{1,0:T(8,128)(2,1)S(1)}, u32[]{:S(2)}, u32[]{:S(2)}) collective-permute-start(bf16[512,1024]{1,0:T(8,128)(2,1)S(1)} %pad_maximum_fusion.7), channel_id=1, source_target_pairs={{0,4},{2,6},{4,0},{6,2},{8,12},{10,14},{12,8},{14,10},{16,20},{18,... | collective-permute-start | bytes 3145736 | tf_op jit(solution)/shard_map/ppermute | solution.py:20
  202.0 42.2 %collective-permute-start.2 = (bf16[2,256,2,384]{3,1,2,0:T(8,128)(2,1)S(1)}, bf16[2,256,2,384]{3,1,2,0:T(8,128)(2,1)S(1)}, u32[]{:S(2)}, u32[]{:S(2)}) collective-permute-start(bf16[2,256,2,384]{3,1,2,0:T(8,128)(2,1)S(1)} %get-tuple-element.42), channel_id=1, source_target_pairs={{0,4},{2,6},{4,0},{6,2},{8,12},{10,14},{12,8},{14,10},{16,20},{18,... | collective-permute-start | bytes 2359304 | tf_op jit(solution)/shard_map/ppermute | solution.py:20
  244.3 26.1 %collective-permute-start.7 = (bf16[512,1024]{1,0:T(8,128)(2,1)S(1)}, bf16[512,1024]{1,0:T(8,128)(2,1)S(1)}, u32[]{:S(2)}, u32[]{:S(2)}) collective-permute-start(bf16[512,1024]{1,0:T(8,128)(2,1)S(1)} %collective-permute-done.5), channel_id=1, source_target_pairs={{0,4},{2,6},{4,0},{6,2},{8,12},{10,14},{12,8},{14,10},{16,20},{18,... | collective-permute-start | bytes 3145736 | tf_op jit(solution)/shard_map/ppermute | solution.py:20
  246.0 46.8 %collective-permute-start.13 = (bf16[512,1024]{1,0:T(8,128)(2,1)S(1)}, bf16[512,1024]{1,0:T(8,128)(2,1)S(1)}, u32[]{:S(2)}, u32[]{:S(2)}) collective-permute-start(bf16[512,1024]{1,0:T(8,128)(2,1)S(1)} %collective-permute-done.11), channel_id=1, source_target_pairs={{0,4},{2,6},{4,0},{6,2},{8,12},{10,14},{12,8},{14,10},{16,20},{18,... | collective-permute-start | bytes 3145736 | tf_op jit(solution)/shard_map/ppermute | solution.py:20
  246.6 88.6 %collective-permute-start.3 = (bf16[4,256,2,384]{3,1,2,0:T(8,128)(2,1)S(1)}, bf16[4,256,2,384]{3,1,2,0:T(8,128)(2,1)S(1)}, u32[]{:S(2)}, u32[]{:S(2)}) collective-permute-start(bf16[4,256,2,384]{3,1,2,0:T(8,128)(2,1)S(1)} %get-tuple-element.40), channel_id=1, source_target_pairs={{0,2},{2,0},{4,6},{6,4},{8,10},{10,8},{12,14},{14,12},{16,18},{18,... | collective-permute-start | bytes 4718600 | tf_op jit(solution)/shard_map/ppermute | solution.py:20
  246.7 68.6 %collective-permute-start.19 = (bf16[512,1024]{1,0:T(8,128)(2,1)S(1)}, bf16[512,1024]{1,0:T(8,128)(2,1)S(1)}, u32[]{:S(2)}, u32[]{:S(2)}) collective-permute-start(bf16[512,1024]{1,0:T(8,128)(2,1)S(1)} %collective-permute-done.17), channel_id=1, source_target_pairs={{0,4},{2,6},{4,0},{6,2},{8,12},{10,14},{12,8},{14,10},{16,20},{18,... | collective-permute-start | bytes 3145736 | tf_op jit(solution)/shard_map/ppermute | solution.py:20
  248.4 86.8 %collective-permute-start.25 = (bf16[512,1024]{1,0:T(8,128)(2,1)S(1)}, bf16[512,1024]{1,0:T(8,128)(2,1)S(1)}, u32[]{:S(2)}, u32[]{:S(2)}) collective-permute-start(bf16[512,1024]{1,0:T(8,128)(2,1)S(1)} %collective-permute-done.23), channel_id=1, source_target_pairs={{0,4},{2,6},{4,0},{6,2},{8,12},{10,14},{12,8},{14,10},{16,20},{18,... | collective-permute-start | bytes 3145736 | tf_op jit(solution)/shard_map/ppermute | solution.py:20
  337.9 86.4 %collective-permute-start.8 = (bf16[384,1024]{1,0:T(8,128)(2,1)S(1)}, bf16[384,1024]{1,0:T(8,128)(2,1)S(1)}, u32[]{:S(2)}, u32[]{:S(2)}) collective-permute-start(bf16[384,1024]{1,0:T(8,128)(2,1)S(1)} %fusion.57), channel_id=1, source_target_pairs={{0,16},{2,18},{4,20},{6,22},{8,24},{10,26},{12,28},{14,30},{16,0},... | collective-permute-start | bytes 2359304 | tf_op jit(solution)/shard_map/ppermute | solution.py:23
  342.2 99.0 %collective-permute-start.14 = (bf16[384,1024]{1,0:T(8,128)(2,1)S(1)}, bf16[384,1024]{1,0:T(8,128)(2,1)S(1)}, u32[]{:S(2)}, u32[]{:S(2)}) collective-permute-start(bf16[384,1024]{1,0:T(8,128)(2,1)S(1)} %fusion.60), channel_id=1, source_target_pairs={{0,16},{2,18},{4,20},{6,22},{8,24},{10,26},{12,28},{14,30},{16,0},... | collective-permute-start | bytes 2359304 | tf_op jit(solution)/shard_map/ppermute | solution.py:23
  344.8 113.2 %collective-permute-start.20 = (bf16[384,1024]{1,0:T(8,128)(2,1)S(1)}, bf16[384,1024]{1,0:T(8,128)(2,1)S(1)}, u32[]{:S(2)}, u32[]{:S(2)}) collective-permute-start(bf16[384,1024]{1,0:T(8,128)(2,1)S(1)} %fusion.63), channel_id=1, source_target_pairs={{0,16},{2,18},{4,20},{6,22},{8,24},{10,26},{12,28},{14,30},{16,0},... | collective-permute-start | bytes 2359304 | tf_op jit(solution)/shard_map/ppermute | solution.py:23
  349.1 124.7 %collective-permute-start.26 = (bf16[384,1024]{1,0:T(8,128)(2,1)S(1)}, bf16[384,1024]{1,0:T(8,128)(2,1)S(1)}, u32[]{:S(2)}, u32[]{:S(2)}) collective-permute-start(bf16[384,1024]{1,0:T(8,128)(2,1)S(1)} %fusion.66), channel_id=1, source_target_pairs={{0,16},{2,18},{4,20},{6,22},{8,24},{10,26},{12,28},{14,30},{16,0},... | collective-permute-start | bytes 2359304 | tf_op jit(solution)/shard_map/ppermute | solution.py:23
  426.2 49.6 %collective-permute-start.9 = (bf16[192,1024]{1,0:T(8,128)(2,1)S(1)}, bf16[192,1024]{1,0:T(8,128)(2,1)S(1)}, u32[]{:S(2)}, u32[]{:S(2)}) collective-permute-start(bf16[192,1024]{1,0:T(8,128)(2,1)S(1)} %dynamic-slice_bitcast_fusion.3), channel_id=1, source_target_pairs={{0,2},{2,0},{4,6},{6,4},{8,10},{10,8},{12,14},{14,12},{16,18},{18,... | collective-permute-start | bytes 1179656 | tf_op jit(solution)/shard_map/ppermute | solution.py:20
  443.0 32.8 %collective-permute-start.15 = (bf16[192,1024]{1,0:T(8,128)(2,1)S(1)}, bf16[192,1024]{1,0:T(8,128)(2,1)S(1)}, u32[]{:S(2)}, u32[]{:S(2)}) collective-permute-start(bf16[192,1024]{1,0:T(8,128)(2,1)S(1)} %dynamic-slice_bitcast_fusion.2), channel_id=1, source_target_pairs={{0,2},{2,0},{4,6},{6,4},{8,10},{10,8},{12,14},{14,12},{16,18},{18,... | collective-permute-start | bytes 1179656 | tf_op jit(solution)/shard_map/ppermute | solution.py:20
  459.9 16.0 %collective-permute-start.21 = (bf16[192,1024]{1,0:T(8,128)(2,1)S(1)}, bf16[192,1024]{1,0:T(8,128)(2,1)S(1)}, u32[]{:S(2)}, u32[]{:S(2)}) collective-permute-start(bf16[192,1024]{1,0:T(8,128)(2,1)S(1)} %dynamic-slice_bitcast_fusion.1), channel_id=1, source_target_pairs={{0,2},{2,0},{4,6},{6,4},{8,10},{10,8},{12,14},{14,12},{16,18},{18,... | collective-permute-start | bytes 1179656 | tf_op jit(solution)/shard_map/ppermute | solution.py:20
  475.7 1.8 collective-permute-start.27
  (27 other events, 125.6 us)
Sparse Core Ops, SparseCore 0:
  10.3 29.8 all-gather.1

commit v2 on v1

v2 whole, which is shorter than its diff:
```python
import functools

import jax
import jax.numpy as jnp
from jax import lax
from jax.experimental import pallas as pl
from jax.experimental.pallas import tpu as pltpu
from jax.sharding import PartitionSpec as P

CAP = 256
CHUNKS = 8
WIDE = 4
MESH = pl.DeviceIdType.MESH


def exchange(ndp, ntp, kept, passed, feats, w_gate, w_up, own_out, other_out, slot_out,
             cots, partial, landed, summed, swapped, weights, grad, grad_in,
             send, recv, high_send, high_recv, y_send, y_recv, weight_sem):
    n_high = ndp // 8
    me = lax.axis_index("dp")
    at = lax.axis_index("tensor")
    core, high = me % 2, me // 8
    core_peer = me + 1 - 2 * core
    x_peer = me + 2 - 4 * ((me // 2) % 2)
    z_peer = me + 4 - 8 * ((me // 4) % 2)
    highs = [((high + s) % n_high) * 8 + me % 8 for s in range(1, n_high)]
    tensors = [(at + s) % ntp for s in range(1, ntp)]
    slots, step = kept.shape[1], kept.shape[2]
    depth = own_out.shape[1]
    block = slot_out.shape[0]
    tile = min(block, 512)

    barrier = pltpu.get_barrier_semaphore()
    for peer in [core_peer, x_peer, z_peer] + highs:
        pl.semaphore_signal(barrier, inc=1, device_id=(peer, at), device_id_type=MESH)
    for peer in tensors:
        pl.semaphore_signal(barrier, inc=1, device_id=(me, peer), device_id_type=MESH)
    pl.semaphore_wait(barrier, 3 + len(highs) + len(tensors))

    def remote(src, dst, send_sem, recv_sem, device):
        return pltpu.make_async_remote_copy(
            src_ref=src, dst_ref=dst, send_sem=send_sem, recv_sem=recv_sem,
            device_id=device, device_id_type=MESH,
        )

    def rows(j, which, count=2):
        return cots.at[j, pl.ds(which * slots, count * slots)]

    def to_core(j):
        return remote(passed.at[j], rows(j, 1, 1), send.at[0, j], recv.at[0, j], (core_peer, at))

    def to_z(j):
        return remote(rows(j, 0), rows(j, 2), send.at[1, j], recv.at[1, j], (z_peer, at))

    def to_x(j):
        return remote(rows(j, 0), rows(j, 4), send.at[2, j], recv.at[2, j], (x_peer, at))

    def on_to_x(j):
        return remote(rows(j, 2), rows(j, 6), send.at[3, j], recv.at[3, j], (x_peer, at))

    def swap(j):
        return remote(
            summed.at[j, 1 - core], swapped.at[j], send.at[4, j], recv.at[4, j], (core_peer, at)
        )

    def to_high(j, s):
        return remote(
            partial.at[s, j], landed.at[s, j], high_send.at[s, j], high_recv.at[s, j],
            (highs[s], at),
        )

    def to_tensor(s):
        start = pl.multiple_of(tensors[s] * block, block)
        return remote(
            grad.at[pl.ds(start, block)], grad_in.at[s], y_send.at[s], y_recv.at[s],
            (me, tensors[s]),
        )

    def weight_copy(i, source):
        columns = pl.ds((i // 2) * step, step)
        return pltpu.make_async_copy(
            source.at[:, columns], weights.at[i % 2], weight_sem.at[i % 2]
        )

    def fetch(i):
        takes_gate = core == i % 2

        @pl.when(takes_gate)
        def _():
            weight_copy(i, w_gate).start()

        @pl.when(jnp.logical_not(takes_gate))
        def _():
            weight_copy(i, w_up).start()

    def grad_turn(i):
        weight_copy(i, w_gate).wait()
        cot = (kept if i % 2 == 0 else passed).at[i // 2]

        def body(k, carry):
            part = pl.ds(pl.multiple_of(k * tile, tile), tile)
            term = lax.dot_general(
                weights[i % 2, part, :], cot[...], (((1,), (1,)), ((), ())),
                preferred_element_type=jnp.float32,
            )
            grad[part, :] = term if i == 0 else grad[part, :] + term
            return carry

        lax.fori_loop(0, grad.shape[0] // tile, body, 0)
        if i + 2 < 2 * CHUNKS:
            fetch(i + 2)

    def multiply(j, s, half):
        return jnp.dot(feats[s, half], cots[j], preferred_element_type=jnp.float32)

    def send_sums(j):
        for s in range(n_high - 1):
            def body(half, carry):
                partial[s, j, half] = multiply(j, s + 1, half).astype(jnp.bfloat16)
                return carry

            lax.fori_loop(0, 2, body, 0)
            to_high(j, s).start()

    def finish(j):
        for s in range(n_high - 1):
            to_high(j, s).wait_recv()

        def body(half, carry):
            total = multiply(j, 0, half)
            for s in range(n_high - 1):
                total += landed[s, j, half].astype(jnp.float32)
            summed[j, half] = total.astype(jnp.bfloat16)
            return carry

        lax.fori_loop(0, 2, body, 0)
        swap(j).start()
        own_out[j] = summed[j, core]

    fetch(0)
    fetch(1)
    for j in range(CHUNKS):
        to_core(j).start()
    for j in range(CHUNKS):
        cots[j, 0:slots] = kept[j]
    for t in range(CHUNKS + 2):
        if t < CHUNKS:
            to_core(t).wait_recv()
            to_z(t).start()
            to_x(t).start()
        if 1 <= t <= CHUNKS:
            to_z(t - 1).wait_recv()
            on_to_x(t - 1).start()
        if t < CHUNKS:
            grad_turn(2 * t)
            grad_turn(2 * t + 1)
        if t == CHUNKS - 1:
            for s in range(ntp - 1):
                to_tensor(s).start()
        if t >= 2:
            to_x(t - 2).wait_recv()
            on_to_x(t - 2).wait_recv()
            send_sums(t - 2)
        if t >= 4:
            finish(t - 4)
    for s in range(ntp - 1):
        to_tensor(s).wait_recv()
    here = pl.ds(pl.multiple_of(at * block, block), block)
    slot = grad[here, :]
    for s in range(ntp - 1):
        slot += grad_in[s]
    slot_out[...] = slot
    for j in range(CHUNKS - 2, CHUNKS):
        finish(j)
    for j in range(CHUNKS):
        swap(j).wait_recv()
        other_out[j] = swapped[j]
        for copy in (to_core(j), to_z(j), to_x(j), on_to_x(j), swap(j)):
            copy.wait_send()
        for s in range(n_high - 1):
            to_high(j, s).wait_send()
    for s in range(ntp - 1):
        to_tensor(s).wait_send()


def on_device(ndp, ntp, tokens, hidden_cot, w_gate, w_up, expert_ids, route_fixed):
    n_high = ndp // 8
    me = lax.axis_index("dp")
    core, x_at, z_low, z_high = me % 2, (me // 2) % 2, (me // 4) % 2, me // 8
    tensor_at = lax.axis_index("tensor")
    is_gate = core == 0

    def flip(value, bit):
        return lax.ppermute(value, "dp", [(i, i ^ bit) for i in range(ndp)])

    def shift_high(value, step):
        return lax.ppermute(value, "dp", [(i, (i + 8 * step) % ndp) for i in range(ndp)])

    def shift_tensor(value, step):
        return lax.ppermute(value, "tensor", [(i, (i + step) % ntp) for i in range(ntp)])

    selected = expert_ids == 0
    routed_flag = jnp.any(selected, axis=1)
    slot_of = jnp.cumsum(routed_flag.astype(jnp.int32)) - 1
    slot_ids = jnp.arange(CAP, dtype=jnp.int32)
    dispatch_mask = (slot_of[None, :] == slot_ids[:, None]) & routed_flag[None, :]
    dispatch = dispatch_mask.astype(jnp.bfloat16)
    dispatch_wide = dispatch_mask.astype(jnp.float32)
    share_all = jnp.sum(jnp.where(selected, route_fixed, 0), axis=1).astype(jnp.float32) / 65536.0
    share = jnp.dot(dispatch_wide, share_all, precision=lax.Precision.HIGHEST)
    routed = jnp.sum(dispatch_wide, axis=1)
    picked = jnp.dot(dispatch, tokens, preferred_element_type=jnp.float32).astype(jnp.bfloat16)
    parts = lax.dynamic_update_index_in_dim(
        jnp.zeros((CAP, ntp, picked.shape[1]), jnp.bfloat16), picked, tensor_at, 1
    )
    for s in range(1, ntp):
        parts = lax.dynamic_update_index_in_dim(
            parts, shift_tensor(picked, s), (tensor_at + ntp - s) % ntp, 1
        )
    gathered = parts.reshape(CAP, -1)
    cot_rows = jnp.dot(dispatch, hidden_cot, preferred_element_type=jnp.float32).astype(
        jnp.bfloat16
    )

    depth = gathered.shape[1] // ndp
    features = gathered.reshape(CAP, n_high, 2, 2, 2 * depth)
    near = lax.dynamic_index_in_dim(features, z_low, 2, keepdims=False)
    far = flip(lax.dynamic_index_in_dim(features, 1 - z_low, 2, keepdims=False), 4)
    both = jnp.stack([near, far])
    here = lax.dynamic_index_in_dim(both, x_at, 3, keepdims=False)
    there = flip(lax.dynamic_index_in_dim(both, 1 - x_at, 3, keepdims=False), 2)
    mine = jnp.concatenate([here, there])
    group = jnp.stack([mine, flip(mine, 1)], axis=1)
    group = group.reshape(8 * CAP, n_high, 2, depth).transpose(1, 2, 3, 0)
    feats = jnp.stack(
        [
            lax.dynamic_index_in_dim(group, (z_high + s) % n_high, 0, keepdims=False)
            for s in range(n_high)
        ]
    )

    width = w_gate.shape[1]
    step = width // CHUNKS

    def cotangents(rows, chunk):
        columns = slice(chunk * (width // WIDE), (chunk + 1) * (width // WIDE))
        gate_pre = jnp.dot(rows, w_gate[:, columns], preferred_element_type=jnp.float32)
        up_pre = jnp.dot(rows, w_up[:, columns], preferred_element_type=jnp.float32)
        sigmoid_gate = jax.nn.sigmoid(gate_pre)
        activated = gate_pre * sigmoid_gate
        hidden = (activated * up_pre).astype(jnp.bfloat16)
        hidden = lax.optimization_barrier(hidden)
        cot_wide = cot_rows[:, columns].astype(jnp.float32)
        route = jnp.sum(hidden.astype(jnp.float32) * cot_wide, axis=1)
        scaled = share[:, None] * cot_wide
        gate_cot = (
            scaled * up_pre * sigmoid_gate * (1.0 + gate_pre * (1.0 - sigmoid_gate))
        ).astype(jnp.bfloat16)
        up_cot = (scaled * activated).astype(jnp.bfloat16)
        return gate_cot, up_cot, route

    kepts, passes, routes = [], [], []
    for chunk in range(WIDE):
        gate_cot, up_cot, route = cotangents(gathered, chunk)
        kept, passed = jnp.where(is_gate, gate_cot, up_cot), jnp.where(is_gate, up_cot, gate_cot)
        for part in range(CHUNKS // WIDE):
            kepts.append(kept[:, part * step : (part + 1) * step])
            passes.append(passed[:, part * step : (part + 1) * step])
        routes.append(route)
    route_sum = sum(routes)
    block = w_gate.shape[0] // ntp
    bf16, f32 = jnp.bfloat16, jnp.float32
    vmem = pl.BlockSpec(memory_space=pltpu.VMEM)
    anywhere = pl.BlockSpec(memory_space=pl.ANY)
    own, other, slot_grad = pl.pallas_call(
        functools.partial(exchange, ndp, ntp),
        out_shape=(
            jax.ShapeDtypeStruct((CHUNKS, depth, step), bf16),
            jax.ShapeDtypeStruct((CHUNKS, depth, step), bf16),
            jax.ShapeDtypeStruct((block, CAP), f32),
        ),
        in_specs=[vmem, vmem, vmem, anywhere, anywhere],
        out_specs=(vmem, vmem, vmem),
        scratch_shapes=[
            pltpu.VMEM((CHUNKS, 8 * CAP, step), bf16),
            pltpu.VMEM((n_high - 1, CHUNKS, 2, depth, step), bf16),
            pltpu.VMEM((n_high - 1, CHUNKS, 2, depth, step), bf16),
            pltpu.VMEM((CHUNKS, 2, depth, step), bf16),
            pltpu.VMEM((CHUNKS, depth, step), bf16),
            pltpu.VMEM((2, w_gate.shape[0], step), bf16),
            pltpu.VMEM((w_gate.shape[0], CAP), f32),
            pltpu.VMEM((ntp - 1, block, CAP), f32),
            pltpu.SemaphoreType.DMA((5, CHUNKS)),
            pltpu.SemaphoreType.DMA((5, CHUNKS)),
            pltpu.SemaphoreType.DMA((n_high - 1, CHUNKS)),
            pltpu.SemaphoreType.DMA((n_high - 1, CHUNKS)),
            pltpu.SemaphoreType.DMA((ntp - 1,)),
            pltpu.SemaphoreType.DMA((ntp - 1,)),
            pltpu.SemaphoreType.DMA((2,)),
        ],
        compiler_params=pltpu.CompilerParams(
            collective_id=0, has_side_effects=True, vmem_limit_bytes=58 * 2**20
        ),
        cost_estimate=pl.CostEstimate(
            flops=26 * 10**9, bytes_accessed=60 * 10**6, transcendentals=0
        ),
    )(jnp.stack(kepts), jnp.stack(passes), feats, w_gate, w_up)
    gate_grad = jnp.where(is_gate, own, other).transpose(1, 0, 2).reshape(depth, width)
    up_grad = jnp.where(is_gate, other, own).transpose(1, 0, 2).reshape(depth, width)

    slot_route = route_sum
    for s in range(1, ntp):
        slot_route += shift_tensor(route_sum, s)
    route_grad = jnp.dot(routed * slot_route, dispatch_wide, precision=lax.Precision.HIGHEST)

    back_dims = (((0,), (0,)), ((), ()))
    token_grad = lax.dot_general(
        dispatch,
        slot_grad.T.astype(jnp.bfloat16),
        back_dims,
        preferred_element_type=jnp.float32,
    ).astype(jnp.bfloat16)
    return token_grad, gate_grad, up_grad, route_grad


def solution(mesh):
    return jax.shard_map(
        functools.partial(on_device, mesh.shape["dp"], mesh.shape["tensor"]),
        mesh=mesh,
        in_specs=(
            P("dp", "tensor"),
            P("dp", "tensor"),
            P(None, "tensor"),
            P(None, "tensor"),
            P("dp", None),
            P("dp", None),
        ),
        out_specs=(P("dp", "tensor"), P("dp", "tensor"), P("dp", "tensor"), P("dp")),
        check_vma=False,
    )
```

time: 496 us -> 350 us (0.71); the launches traced: 487 us -> 349 us
  waiting for transfers between devices: 322 us -> 35.5 us
  Pallas kernels: 0 us -> 221 us
  matrix products: 93.7 us -> 49.4 us
  starting transfers between devices: 23.3 us -> 8.09 us
  between operations: 15.2 us -> 1.1 us
  local copies, waits for them, and re-layouts: 19.6 us -> 26 us
    pallas_call x0 -> x1, Pallas kernels: none -> 221 us  [on_device(): pl.pallas_call(functools.partial(exchange, ndp, ntp), out_shape=(jax.Shap...]
    ppermute x23 -> x3, waiting for transfers between devices: 175 us -> 23.7 us  [flip(): return lax.ppermute(value, 'dp', [(i, i ^ bit) for i in range(ndp)])]
    ppermute x4 -> x0, waiting for transfers between devices: 118 us -> none  [shift_high(): lax.ppermute(value, 'dp', [(i, (i + 8 * step) % ndp) for i in range(ndp)])]
    dot_general x18 -> x8, matrix products: 85.8 us -> 40.8 us  [the longest x4 21.8 us: cotangents(): jnp.dot(rows, w_gate[:, columns], preferred_element_type=jnp.float32)]
    all_gather x1 -> x0, waiting for transfers between devices: 25.9 us -> none  [on_device(): gathered = lax.all_gather(picked, 'tensor', axis=1, tiled=True)]
    ppermute x23 -> x3, starting transfers between devices: 16.2 us -> 3.26 us  [flip(): return lax.ppermute(value, 'dp', [(i, i ^ bit) for i in range(ndp)])]
    ppermute x2, waiting for transfers between devices: 1.98 us -> 11.8 us  [shift_tensor(): lax.ppermute(value, 'tensor', [(i, (i + step) % ntp) for i in range(ntp)])]
    concatenate x5 -> x0, other arithmetic: 6.39 us -> none  [the longest x4 4.6 us: on_device(): jnp.concatenate([kept, flip(jnp.where(is_gate, up_cot, gate_cot), 1)])]
  transfers between devices with their start and end apart: 30 -> 5, of which waited for: 17 -> 4; matrix products, arithmetic and copies ran while one was open for 15% -> 5% of each run, Pallas kernels for 0% -> 0%
where the time goes in v2:
time: 350 us; the launch traced here: 349 us
  Pallas kernels  221 us (63%)
  matrix products  49.4 us (14%)
  waiting for transfers between devices  35.5 us (10%)
  local copies, waits for them, and re-layouts  26 us (7%)
  other arithmetic  8.67 us (2%)
  starting transfers between devices  8.09 us (2%)
    pallas_call x1, Pallas kernels, on_device(): pl.pallas_call(functools.partial(exchange, ndp, ntp), out_shape=(jax.Shap...  221 us
    ppermute x3, waiting for transfers between devices, flip(): return lax.ppermute(value, 'dp', [(i, i ^ bit) for i in range(ndp)])  23.7 us
    dot_general x4, matrix products, cotangents(): jnp.dot(rows, w_gate[:, columns], preferred_element_type=jnp.float32)  21.8 us
    dot_general x4, matrix products, cotangents(): up_pre = jnp.dot(rows, w_up[:, columns], preferred_element_type=jnp.float32)  19 us
    ppermute x2, waiting for transfers between devices, shift_tensor(): lax.ppermute(value, 'tensor', [(i, (i + step) % ntp) for i in range(ntp)])  11.8 us
    unnamed x41, local copies, waits for them, and re-layouts  8.17 us
  transfers between devices with their start and end apart: 5, of which 4 were waited for; matrix products, arithmetic and copies ran while one was open for 5% of the time, Pallas kernels for 0%

profile of v2, /device:TPU:0, one launch (start us, length us, event | category | flops | bytes accessed | tf_op | source)
XLA Modules:
  0.0 349.4 jit_solution(11551920532747653598)
XLA Ops:
  2.7 3.0 collective-permute-start
  6.8 4.8 %convolution_convert_fusion = bf16[256,4096]{1,0:T(8,128)(2,1)} fusion(bf16[512,4096]{1,0:T(8,128)(2,1)} %param.7, s32[512]{0:T(512)S(1)} %add_bitcast_fusion, pred[512]{0:T(512)(128)(4,1)S(1)} %fusion.88), kind=kOutput, calls=%fused_computation.16 | convolution fusion | flops 1075052544 | bytes 6294016 | tf_op jit(solution)/shard_map/dot_general | solution.py:221
  11.6 11.8 %collective-permute-done = bf16[256,1536]{1,0:T(8,128)(2,1)} collective-permute-done((bf16[256,1536]{1,0:T(8,128)(2,1)S(1)}, bf16[256,1536]{1,0:T(8,128)(2,1)}, u32[]{:S(2)}, u32[]{:S(2)}) %collective-permute-start) | collective-permute-done | bytes 786464 | tf_op jit(solution)/shard_map/ppermute | solution.py:200
  23.4 1.4 copy.21
  24.8 4.6 %fusion.4 = f32[256,1024]{1,0:T(8,128)S(1)} fusion(bf16[256,3072]{0,1:T(8,128)(2,1)S(1)} %bitcast.112, bf16[3072,4096]{1,0:T(8,128)(2,1)} %w_gate.1), kind=kOutput, calls=%fused_computation.4 | convolution fusion | flops 1610612736 | bytes 8912896 | tf_op jit(solution)/shard_map/dot_general | solution.py:247
  29.4 4.6 %fusion.8 = f32[256,1024]{1,0:T(8,128)S(1)} fusion(bf16[256,3072]{0,1:T(8,128)(2,1)S(1)} %bitcast.113, bf16[3072,4096]{1,0:T(8,128)(2,1)} %w_gate.1), kind=kOutput, calls=%fused_computation.8 | convolution fusion | flops 1610612736 | bytes 8912896 | tf_op jit(solution)/shard_map/dot_general | solution.py:247
  34.1 4.6 %fusion.12 = f32[256,1024]{1,0:T(8,128)S(1)} fusion(bf16[256,3072]{0,1:T(8,128)(2,1)S(1)} %bitcast.114, bf16[3072,4096]{1,0:T(8,128)(2,1)} %w_gate.1), kind=kOutput, calls=%fused_computation.12 | convolution fusion | flops 1610612736 | bytes 8912896 | tf_op jit(solution)/shard_map/dot_general | solution.py:247
  38.7 4.6 %fusion.2 = f32[256,1024]{1,0:T(8,128)S(1)} fusion(bf16[256,3072]{0,1:T(8,128)(2,1)S(1)} %bitcast.115, bf16[3072,4096]{1,0:T(8,128)(2,1)} %w_up.1), kind=kOutput, calls=%fused_computation.2 | convolution fusion | flops 1610612736 | bytes 8912896 | tf_op jit(solution)/shard_map/dot_general | solution.py:248
  43.3 4.7 %multiply_convert_fusion.1 = (bf16[256,1024]{1,0:T(8,128)(2,1)S(1)}, f32[256,1024]{1,0:T(8,128)S(1)}) fusion(f32[256,1024]{1,0:T(8,128)S(1)} %fusion.4, bf16[256,3072]{0,1:T(8,128)(2,1)S(1)} %bitcast.116, bf16[3072,4096]{1,0:T(8,128)(2,1)} %w_up.1), kind=kOutput, calls=%fused_computation.67 | convolution fusion | flops 1612185600 | bytes 10485760 | tf_op jit(solution)/shard_map/dot_general | solution.py:248
  48.0 4.7 %multiply_convert_fusion.2 = (bf16[256,1024]{1,0:T(8,128)(2,1)S(1)}, f32[256,1024]{1,0:T(8,128)S(1)}) fusion(f32[256,1024]{1,0:T(8,128)S(1)} %fusion.8, bf16[256,3072]{0,1:T(8,128)(2,1)S(1)} %bitcast.117, bf16[3072,4096]{1,0:T(8,128)(2,1)} %w_up.1), kind=kOutput, calls=%fused_computation.68 | convolution fusion | flops 1612185600 | bytes 10485760 | tf_op jit(solution)/shard_map/dot_general | solution.py:248
  52.7 5.0 %multiply_convert_fusion.3 = (bf16[256,1024]{1,0:T(8,128)(2,1)S(1)}, f32[256,1024]{1,0:T(8,128)S(1)}) fusion(f32[256,1024]{1,0:T(8,128)S(1)} %fusion.12, bf16[256,3072]{0,1:T(8,128)(2,1)S(1)} %bitcast.118, bf16[3072,4096]{1,0:T(8,128)(2,1)} %w_up.1), kind=kOutput, calls=%fused_computation.69 | convolution fusion | flops 1612185600 | bytes 10485760 | tf_op jit(solution)/shard_map/dot_general | solution.py:248
  57.7 8.0 %broadcast_select_fusion = (bf16[256,1024]{1,0:T(8,128)(2,1)}, bf16[256,1024]{1,0:T(8,128)(2,1)}, bf16[256,1024]{1,0:T(8,128)(2,1)}, bf16[256,1024]{1,0:T(8,128)...) fusion(pred[]{:T(512)S(6)} %eq.34, ...), kind=kOutput, calls=%fused_computation.89 | convolution fusion | flops 1627389952 | bytes 24642560 | tf_op jit(solution)/shard_map/dot_general | solution.py:247
  66.7 1.8 collective-permute-start.4
  68.9 1.6 collective-permute-start.1
  71.5 1.0 fusion.68
  74.5 1.4 copy-done.9
  76.3 1.7 fusion.63
  78.0 1.7 fusion.62.passed
  79.6 1.3 broadcast_select_fusion.6
  81.0 6.2 %collective-permute-done.1 = bf16[256,2,2,384]{3,0,2,1:T(8,128)(2,1)S(1)} collective-permute-done((bf16[256,2,2,384]{3,0,2,1:T(8,128)(2,1)S(1)}, bf16[256,2,2,384]{3,0,2,1:T(8,128)(2,1)S(1)}, u32[]{:S(2)}, u32[]{:S(2)}) %collective-permute-start.1) | collective-permute-done | bytes 786464 | tf_op jit(solution)/shard_map/ppermute | solution.py:194
  87.3 1.5 collective-permute-start.2
  89.2 15.4 %collective-permute-done.2 = bf16[2,256,2,384]{3,1,2,0:T(8,128)(2,1)S(1)} collective-permute-done((bf16[2,256,2,384]{3,1,2,0:T(8,128)(2,1)S(1)}, bf16[2,256,2,384]{3,1,2,0:T(8,128)(2,1)S(1)}, u32[]{:S(2)}, u32[]{:S(2)}) %collective-permute-start.2) | collective-permute-done | bytes 786464 | tf_op jit(solution)/shard_map/ppermute | solution.py:194
  105.1 1.1 fusion.54
  106.2 2.1 collective-permute-done.3
  108.7 5.9 %copy.24 = bf16[4,2,256,2,384]{2,1,0,4,3:T(2,128)(2,1)} copy(bf16[4,2,256,2,384]{4,2,3,1,0:T(8,128)(2,1)S(1)} %pad_maximum_fusion) | data formatting | bytes 6291456 | tf_op jit(solution)/shard_map/stack | solution.py:233
  114.6 4.8 %reshape.52 = bf16[2048,2,2,192]{0,3,2,1:T(8,128)(2,1)S(1)} reshape(bf16[4,2,256,2,384]{2,1,0,4,3:T(2,128)(2,1)} %copy.24) | data formatting | bytes 6291456 | tf_op jit(solution)/shard_map/reshape | solution.py:234
  119.6 1.9 pad_maximum_fusion.1.feats
  121.6 220.7 %shard_map.93 = (bf16[8,192,512]{2,1,0:T(8,128)(2,1)}, bf16[8,192,512]{2,1,0:T(8,128)(2,1)}, f32[1536,256]{1,0:T(8,128)}) custom-call(bf16[8,256,512]{2,1,0:T(8,128)(2,1)} %copy-done.10, bf16[8,256,512]{2,1,0:T(8,128)(2,1)} %fusion.62.passed, bf16[2,2,192,2048]{3,2,1,0:T(8,128)(2,1)} %pad_maximum_fusion.1.feats, bf16[3072,4096]{1,0:T(8,128)(2,1)} %w_gate.1, ...), custom_call_target="tpu_custom_call" | custom-call | flops 25999998976 | bytes 60000000 | tf_op jit(solution)/shard_map/pallas_call | solution.py:275
  342.3 2.1 select_bitcast_fusion
  344.4 1.3 copy.28
  345.7 1.3 copy.29
  347.7 1.8 convolution_convert_fusion.1
  (68 shorter events, 9.9 us)
Async XLA Ops:
  0.6 1.5 copy-start
  0.6 5.1 %copy-start.11 = (s32[512,2]{0,1:T(2,128)S(1)}, s32[512,2]{0,1:T(2,128)}, u32[]{:S(2)}) copy-start(s32[512,2]{0,1:T(2,128)} %param.10) | copy-start | bytes 12292
  0.7 5.1 %copy-start.12 = (s32[512,2]{0,1:T(2,128)S(1)}, s32[512,2]{0,1:T(2,128)}, u32[]{:S(2)}) copy-start(s32[512,2]{0,1:T(2,128)} %param.11) | copy-start | bytes 12292
  2.7 20.7 %collective-permute-start = (bf16[256,1536]{1,0:T(8,128)(2,1)S(1)}, bf16[256,1536]{1,0:T(8,128)(2,1)}, u32[]{:S(2)}, u32[]{:S(2)}) collective-permute-start(bf16[256,1536]{1,0:T(8,128)(2,1)S(1)} %convolution_convert_fusion.2), channel_id=1, source_target_pairs={{0,1},{1,0},{2,3},{3,2},{4,5},{5,4},{6,7},{7,6},{8,9},{9,8},{10,11... | collective-permute-start | bytes 2359304 | tf_op jit(solution)/shard_map/ppermute | solution.py:200
  52.7 5.1 %copy-start.2 = (bf16[256,4096]{1,0:T(8,128)(2,1)S(1)}, bf16[256,4096]{1,0:T(8,128)(2,1)}, u32[]{:S(2)}) copy-start(bf16[256,4096]{1,0:T(8,128)(2,1)} %convolution_convert_fusion) | copy-start | bytes 6291460
  66.7 38.4 %collective-permute-start.4 = (f32[256]{0:T(256)S(1)}, f32[256]{0:T(256)S(1)}, u32[]{:S(2)}, u32[]{:S(2)}) collective-permute-start(f32[256]{0:T(256)S(1)} %add_add_fusion), channel_id=1, source_target_pairs={{0,1},{1,0},{2,3},{3,2},{4,5},{5,4},{6,7},{7,6},{8,9},{9,8},{10,11... | collective-permute-start | bytes 3080 | tf_op jit(solution)/shard_map/ppermute | solution.py:200
  68.6 5.9 %copy-start.4 = (bf16[256,1024]{1,0:T(8,128)(2,1)S(1)}, bf16[256,1024]{1,0:T(8,128)(2,1)}, u32[]{:S(2)}) copy-start(bf16[256,1024]{1,0:T(8,128)(2,1)} %get-tuple-element.36) | copy-start | bytes 1572868
  68.9 18.2 %collective-permute-start.1 = (bf16[256,2,2,384]{3,0,2,1:T(8,128)(2,1)S(1)}, bf16[256,2,2,384]{3,0,2,1:T(8,128)(2,1)S(1)}, u32[]{:S(2)}, u32[]{:S(2)}) collective-permute-start(bf16[256,2,2,384]{3,0,2,1:T(8,128)(2,1)S(1)} %bitcast.126), channel_id=1, source_target_pairs={{0,8},{2,10},{4,12},{6,14},{8,0},{10,2},{12,4},{14,6},{16,24},{18,... | collective-permute-start | bytes 2359304 | tf_op jit(solution)/shard_map/ppermute | solution.py:194
  74.5 1.4 copy-start.9
  87.1 1.8 copy-start.5
  87.1 1.8 copy-start.6
  87.1 1.8 copy-start.7
  87.1 1.9 copy-start.8
  87.3 17.3 %collective-permute-start.2 = (bf16[2,256,2,384]{3,1,2,0:T(8,128)(2,1)S(1)}, bf16[2,256,2,384]{3,1,2,0:T(8,128)(2,1)S(1)}, u32[]{:S(2)}, u32[]{:S(2)}) collective-permute-start(bf16[2,256,2,384]{3,1,2,0:T(8,128)(2,1)S(1)} %get-tuple-element.42), channel_id=1, source_target_pairs={{0,4},{2,6},{4,0},{6,2},{8,12},{10,14},{12,8},{14,10},{16,20},{18,... | collective-permute-start | bytes 2359304 | tf_op jit(solution)/shard_map/ppermute | solution.py:194
  104.9 3.5 collective-permute-start.3
  105.1 3.3 copy-start.10
  345.7 2.0 copy-start.3
  345.7 3.8 %copy-start.1 = (bf16[512,1536]{1,0:T(8,128)(2,1)S(1)}, bf16[512,1536]{1,0:T(8,128)(2,1)}, u32[]{:S(2)}) copy-start(bf16[512,1536]{1,0:T(8,128)(2,1)} %param.6) | copy-start | bytes 4718596

commit v3 on v2

--- a/solution.py
+++ b/solution.py
@@ -10,12 +10,14 @@
 CAP = 256
 CHUNKS = 8
 WIDE = 4
+BY_Z = 3
 MESH = pl.DeviceIdType.MESH
 
 
-def exchange(ndp, ntp, kept, passed, feats, w_gate, w_up, own_out, other_out, slot_out,
-             cots, partial, landed, summed, swapped, weights, grad, grad_in,
-             send, recv, high_send, high_recv, y_send, y_recv, weight_sem):
+def exchange(ndp, ntp, feats, w_gate, w_up, *refs):
+    kept_parts, passed_parts, refs = refs[:WIDE], refs[WIDE : 2 * WIDE], refs[2 * WIDE :]
+    (own_out, other_out, slot_out, cots, partial, landed, summed, swapped, weights, grad, grad_in,
+     send, recv, high_send, high_recv, y_send, y_recv, weight_sem) = refs
     n_high = ndp // 8
     me = lax.axis_index("dp")
     at = lax.axis_index("tensor")
@@ -25,7 +27,15 @@
     z_peer = me + 4 - 8 * ((me // 4) % 2)
     highs = [((high + s) % n_high) * 8 + me % 8 for s in range(1, n_high)]
     tensors = [(at + s) % ntp for s in range(1, ntp)]
-    slots, step = kept.shape[1], kept.shape[2]
+    slots, step = cots.shape[1] // 8, cots.shape[2]
+    halves = CHUNKS // WIDE
+
+    def kept(j):
+        return kept_parts[j // halves].at[:, pl.ds(j % halves * step, step)]
+
+    def passed(j):
+        return passed_parts[j // halves].at[:, pl.ds(j % halves * step, step)]
+
     depth = own_out.shape[1]
     block = slot_out.shape[0]
     tile = min(block, 512)
@@ -47,7 +57,7 @@
         return cots.at[j, pl.ds(which * slots, count * slots)]
 
     def to_core(j):
-        return remote(passed.at[j], rows(j, 1, 1), send.at[0, j], recv.at[0, j], (core_peer, at))
+        return remote(passed(j), rows(j, 1, 1), send.at[0, j], recv.at[0, j], (core_peer, at))
 
     def to_z(j):
         return remote(rows(j, 0), rows(j, 2), send.at[1, j], recv.at[1, j], (z_peer, at))
@@ -55,7 +65,9 @@
     def to_x(j):
         return remote(rows(j, 0), rows(j, 4), send.at[2, j], recv.at[2, j], (x_peer, at))
 
-    def on_to_x(j):
+    def onward(j):
+        if j == BY_Z:
+            return remote(rows(j, 4), rows(j, 6), send.at[3, j], recv.at[3, j], (z_peer, at))
         return remote(rows(j, 2), rows(j, 6), send.at[3, j], recv.at[3, j], (x_peer, at))
 
     def swap(j):
@@ -95,7 +107,7 @@
 
     def grad_turn(i):
         weight_copy(i, w_gate).wait()
-        cot = (kept if i % 2 == 0 else passed).at[i // 2]
+        cot = (kept if i % 2 == 0 else passed)(i // 2)
 
         def body(k, carry):
             part = pl.ds(pl.multiple_of(k * tile, tile), tile)
@@ -142,15 +154,15 @@
     for j in range(CHUNKS):
         to_core(j).start()
     for j in range(CHUNKS):
-        cots[j, 0:slots] = kept[j]
+        cots[j, 0:slots] = kept(j)[...]
     for t in range(CHUNKS + 2):
-        if t < CHUNKS:
-            to_core(t).wait_recv()
-            to_z(t).start()
-            to_x(t).start()
         if 1 <= t <= CHUNKS:
-            to_z(t - 1).wait_recv()
-            on_to_x(t - 1).start()
+            (to_x if t - 1 == BY_Z else to_z)(t - 1).wait_recv()
+            onward(t - 1).start()
+        for j in range(0 if t == 0 else t + 1, min(t + 2, CHUNKS)):
+            to_core(j).wait_recv()
+            to_z(j).start()
+            to_x(j).start()
         if t < CHUNKS:
             grad_turn(2 * t)
             grad_turn(2 * t + 1)
@@ -158,8 +170,8 @@
             for s in range(ntp - 1):
                 to_tensor(s).start()
         if t >= 2:
-            to_x(t - 2).wait_recv()
-            on_to_x(t - 2).wait_recv()
+            (to_z if t - 2 == BY_Z else to_x)(t - 2).wait_recv()
+            onward(t - 2).wait_recv()
             send_sums(t - 2)
         if t >= 4:
             finish(t - 4)
@@ -175,7 +187,7 @@
     for j in range(CHUNKS):
         swap(j).wait_recv()
         other_out[j] = swapped[j]
-        for copy in (to_core(j), to_z(j), to_x(j), on_to_x(j), swap(j)):
+        for copy in (to_core(j), to_z(j), to_x(j), onward(j), swap(j)):
             copy.wait_send()
         for s in range(n_high - 1):
             to_high(j, s).wait_send()
@@ -226,18 +238,11 @@
     features = gathered.reshape(CAP, n_high, 2, 2, 2 * depth)
     near = lax.dynamic_index_in_dim(features, z_low, 2, keepdims=False)
     far = flip(lax.dynamic_index_in_dim(features, 1 - z_low, 2, keepdims=False), 4)
-    both = jnp.stack([near, far])
-    here = lax.dynamic_index_in_dim(both, x_at, 3, keepdims=False)
-    there = flip(lax.dynamic_index_in_dim(both, 1 - x_at, 3, keepdims=False), 2)
-    mine = jnp.concatenate([here, there])
-    group = jnp.stack([mine, flip(mine, 1)], axis=1)
-    group = group.reshape(8 * CAP, n_high, 2, depth).transpose(1, 2, 3, 0)
-    feats = jnp.stack(
-        [
-            lax.dynamic_index_in_dim(group, (z_high + s) % n_high, 0, keepdims=False)
-            for s in range(n_high)
-        ]
-    )
+
+    def cross(far):
+        both = jnp.stack([near, far])
+        here = lax.dynamic_index_in_dim(both, x_at, 3, keepdims=False)
+        return here, flip(lax.dynamic_index_in_dim(both, 1 - x_at, 3, keepdims=False), 2)
 
     width = w_gate.shape[1]
     step = width // CHUNKS
@@ -260,13 +265,26 @@
         return gate_cot, up_cot, route
 
     kepts, passes, routes = [], [], []
+    tied = gathered
     for chunk in range(WIDE):
-        gate_cot, up_cot, route = cotangents(gathered, chunk)
-        kept, passed = jnp.where(is_gate, gate_cot, up_cot), jnp.where(is_gate, up_cot, gate_cot)
-        for part in range(CHUNKS // WIDE):
-            kepts.append(kept[:, part * step : (part + 1) * step])
-            passes.append(passed[:, part * step : (part + 1) * step])
+        if chunk == 2:
+            tied, far = lax.optimization_barrier((tied, far))
+            here, there = cross(far)
+        if chunk == 3:
+            tied, there = lax.optimization_barrier((tied, there))
+        gate_cot, up_cot, route = cotangents(tied, chunk)
+        kepts.append(jnp.where(is_gate, gate_cot, up_cot))
+        passes.append(jnp.where(is_gate, up_cot, gate_cot))
         routes.append(route)
+    mine = jnp.concatenate([here, there])
+    group = jnp.stack([mine, flip(mine, 1)], axis=1)
+    group = group.reshape(8 * CAP, n_high, 2, depth).transpose(1, 2, 3, 0)
+    feats = jnp.stack(
+        [
+            lax.dynamic_index_in_dim(group, (z_high + s) % n_high, 0, keepdims=False)
+            for s in range(n_high)
+        ]
+    )
     route_sum = sum(routes)
     block = w_gate.shape[0] // ntp
     bf16, f32 = jnp.bfloat16, jnp.float32
@@ -279,7 +297,7 @@
             jax.ShapeDtypeStruct((CHUNKS, depth, step), bf16),
             jax.ShapeDtypeStruct((block, CAP), f32),
         ),
-        in_specs=[vmem, vmem, vmem, anywhere, anywhere],
+        in_specs=[vmem, anywhere, anywhere] + [vmem] * (2 * WIDE),
         out_specs=(vmem, vmem, vmem),
         scratch_shapes=[
             pltpu.VMEM((CHUNKS, 8 * CAP, step), bf16),
@@ -304,7 +322,7 @@
         cost_estimate=pl.CostEstimate(
             flops=26 * 10**9, bytes_accessed=60 * 10**6, transcendentals=0
         ),
-    )(jnp.stack(kepts), jnp.stack(passes), feats, w_gate, w_up)
+    )(feats, w_gate, w_up, *kepts, *passes)
     gate_grad = jnp.where(is_gate, own, other).transpose(1, 0, 2).reshape(depth, width)
     up_grad = jnp.where(is_gate, other, own).transpose(1, 0, 2).reshape(depth, width)
 

time: 350 us -> 329 us (0.940)
  Pallas kernels: 221 us -> 209 us
  local copies, waits for them, and re-layouts: 26 us -> 19.4 us
  waiting for transfers between devices: 35.5 us -> 30.6 us
    pallas_call x1, Pallas kernels: 221 us -> 209 us  [on_device(): pl.pallas_call(functools.partial(exchange, ndp, ntp), out_shape=(jax.Shap...]
    unnamed x41 -> x16, local copies, waits for them, and re-layouts: 8.17 us -> 2.17 us
    ppermute x3, waiting for transfers between devices: 23.7 us -> 18.6 us  [flip(): return lax.ppermute(value, 'dp', [(i, i ^ bit) for i in range(ndp)])]
  transfers between devices with their start and end apart: 5 -> 5, of which waited for: 4 -> 4; matrix products, arithmetic and copies ran while one was open for 5% -> 10% of each run, Pallas kernels for 0% -> 0%
where the time goes in v3:
time: 329 us; the launch traced here: 328 us
  Pallas kernels  209 us (64%)
  matrix products  50.6 us (15%)
  waiting for transfers between devices  30.6 us (9%)
  local copies, waits for them, and re-layouts  19.4 us (6%)
  other arithmetic  10.6 us (3%)
  starting transfers between devices  7.51 us (2%)
    pallas_call x1, Pallas kernels, on_device(): pl.pallas_call(functools.partial(exchange, ndp, ntp), out_shape=(jax.Shap...  209 us
    dot_general x4, matrix products, cotangents(): jnp.dot(rows, w_gate[:, columns], preferred_element_type=jnp.float32)  23 us
    dot_general x4, matrix products, cotangents(): up_pre = jnp.dot(rows, w_up[:, columns], preferred_element_type=jnp.float32)  19.2 us
    ppermute x3, waiting for transfers between devices, flip(): return lax.ppermute(value, 'dp', [(i, i ^ bit) for i in range(ndp)])  18.6 us
    ppermute x2, waiting for transfers between devices, shift_tensor(): lax.ppermute(value, 'tensor', [(i, (i + step) % ntp) for i in range(ntp)])  12 us
  transfers between devices with their start and end apart: 5, of which 4 were waited for; matrix products, arithmetic and copies ran while one was open for 10% of the time, Pallas kernels for 0%

profile of v3, /device:TPU:0, one launch (start us, length us, event | category | flops | bytes accessed | tf_op | source)
XLA Modules:
  0.0 328.1 jit_solution(243640473383908840)
XLA Ops:
  0.7 0.8 fusion.72
  2.7 3.0 collective-permute-start
  6.8 4.8 %convolution_convert_fusion = bf16[256,4096]{1,0:T(8,128)(2,1)} fusion(bf16[512,4096]{1,0:T(8,128)(2,1)} %param.7, s32[512]{0:T(512)S(1)} %add_bitcast_fusion, pred[512]{0:T(512)(128)(4,1)S(1)} %fusion.72), kind=kOutput, calls=%fused_computation.16 | convolution fusion | flops 1075052544 | bytes 6294016 | tf_op jit(solution)/shard_map/dot_general | solution.py:233
  11.6 11.8 %collective-permute-done = bf16[256,1536]{1,0:T(8,128)(2,1)} collective-permute-done((bf16[256,1536]{1,0:T(8,128)(2,1)S(1)}, bf16[256,1536]{1,0:T(8,128)(2,1)}, u32[]{:S(2)}, u32[]{:S(2)}) %collective-permute-start) | collective-permute-done | bytes 786464 | tf_op jit(solution)/shard_map/ppermute | solution.py:212
  23.4 1.4 copy.32
  24.8 5.6 %fusion.8 = f32[256,1024]{1,0:T(8,128)} fusion(bf16[256,3072]{0,1:T(8,128)(2,1)S(1)} %bitcast.48, bf16[3072,4096]{1,0:T(8,128)(2,1)} %w_gate.1), kind=kOutput, calls=%fused_computation.8 | convolution fusion | flops 1610612736 | bytes 8912896 | tf_op jit(solution)/shard_map/dot_general | solution.py:252
  30.4 5.6 %fusion.12 = f32[256,1024]{1,0:T(8,128)} fusion(bf16[256,3072]{0,1:T(8,128)(2,1)S(1)} %bitcast.49, bf16[3072,4096]{1,0:T(8,128)(2,1)} %w_gate.1), kind=kOutput, calls=%fused_computation.12 | convolution fusion | flops 1610612736 | bytes 8912896 | tf_op jit(solution)/shard_map/dot_general | solution.py:252
  36.1 1.2 copy.34
  37.3 1.8 collective-permute-start.1
  39.4 5.0 %multiply_convert_fusion.3 = (bf16[256,1024]{1,0:T(8,128)(2,1)S(1)}, f32[256,1024]{1,0:T(8,128)S(1)}) fusion(f32[256,1024]{1,0:T(8,128)} %fusion.12, bf16[256,3072]{0,1:T(8,128)(2,1)S(1)} %bitcast.51, bf16[3072,4096]{1,0:T(8,128)(2,1)} %w_up.1), kind=kOutput, calls=%fused_computation.69 | convolution fusion | flops 1612185600 | bytes 10485760 | tf_op jit(solution)/shard_map/dot_general | solution.py:253
  44.5 4.7 %multiply_convert_fusion.2 = (bf16[256,1024]{1,0:T(8,128)(2,1)S(1)}, f32[256,1024]{1,0:T(8,128)S(1)}) fusion(f32[256,1024]{1,0:T(8,128)S(1)} %copy-done.6, bf16[256,3072]{0,1:T(8,128)(2,1)S(1)} %bitcast.52, bf16[3072,4096]{1,0:T(8,128)(2,1)} %w_up.1), kind=kOutput, calls=%fused_computation.68 | convolution fusion | flops 1612185600 | bytes 10485760 | tf_op jit(solution)/shard_map/dot_general | solution.py:253
  49.2 7.1 %collective-permute-done.1 = bf16[256,2,2,384]{3,0,2,1:T(8,128)(2,1)} collective-permute-done((bf16[256,2,2,384]{3,0,2,1:T(8,128)(2,1)}, bf16[256,2,2,384]{3,0,2,1:T(8,128)(2,1)}, u32[]{:S(2)}, u32[]{:S(2)}) %collective-permute-start.1) | collective-permute-done | bytes 786464 | tf_op jit(solution)/shard_map/ppermute | solution.py:206
  56.3 4.6 %fusion.4 = f32[256,1024]{1,0:T(8,128)S(1)} fusion(bf16[256,3072]{0,1:T(8,128)(2,1)S(1)} %bitcast.53, bf16[3072,4096]{1,0:T(8,128)(2,1)} %w_gate.1), kind=kOutput, calls=%fused_computation.4 | convolution fusion | flops 1610612736 | bytes 8912896 | tf_op jit(solution)/shard_map/dot_general | solution.py:252
  60.9 1.3 fusion.51
  62.2 1.5 collective-permute-start.2
  63.7 4.9 %multiply_convert_fusion.1 = (bf16[256,1024]{1,0:T(8,128)(2,1)S(1)}, f32[256,1024]{1,0:T(8,128)S(1)}) fusion(f32[256,1024]{1,0:T(8,128)S(1)} %fusion.4, bf16[256,3072]{0,1:T(8,128)(2,1)S(1)} %bitcast.54, bf16[3072,4096]{1,0:T(8,128)(2,1)} %w_up.1), kind=kOutput, calls=%fused_computation.67 | convolution fusion | flops 1612185600 | bytes 10485760 | tf_op jit(solution)/shard_map/dot_general | solution.py:253
  68.6 11.5 %collective-permute-done.2 = bf16[2,256,2,384]{3,1,2,0:T(8,128)(2,1)S(1)} collective-permute-done((bf16[2,256,2,384]{3,1,2,0:T(8,128)(2,1)S(1)}, bf16[2,256,2,384]{3,1,2,0:T(8,128)(2,1)S(1)}, u32[]{:S(2)}, u32[]{:S(2)}) %collective-permute-start.2) | collective-permute-done | bytes 786464 | tf_op jit(solution)/shard_map/ppermute | solution.py:206
  80.1 4.6 %fusion.2 = f32[256,1024]{1,0:T(8,128)S(1)} fusion(bf16[256,3072]{0,1:T(8,128)(2,1)S(1)} %bitcast.55, bf16[3072,4096]{1,0:T(8,128)(2,1)} %w_up.1), kind=kOutput, calls=%fused_computation.2 | convolution fusion | flops 1610612736 | bytes 8912896 | tf_op jit(solution)/shard_map/dot_general | solution.py:253
  85.1 1.2 copy-done.2
  86.5 7.2 %broadcast_select_fusion = (bf16[256,1024]{1,0:T(8,128)(2,1)}, bf16[256,1024]{1,0:T(8,128)(2,1)S(1)}, bf16[256,1024]{1,0:T(8,128)(2,1)S(1)}, bf16[256,1024]{1,0:...) fusion(pred[]{:T(512)S(6)} %eq.34, ...), kind=kOutput, calls=%fused_computation.89 | convolution fusion | flops 1627389952 | bytes 24642560 | tf_op jit(solution)/shard_map/dot_general | solution.py:252
  94.7 1.2 collective-permute-start.4
  95.9 1.1 broadcast_select_fusion.4
  96.9 1.2 broadcast_select_fusion.6
  98.3 0.9 fusion.54
  99.6 6.0 %copy.35 = bf16[4,2,256,2,384]{2,1,0,4,3:T(2,128)(2,1)} copy(bf16[4,2,256,2,384]{4,2,3,1,0:T(8,128)(2,1)S(1)} %pad_maximum_fusion) | data formatting | bytes 6291456 | tf_op jit(solution)/shard_map/stack | solution.py:280
  105.5 4.8 %reshape.52 = bf16[2048,2,2,192]{0,3,2,1:T(8,128)(2,1)S(1)} reshape(bf16[4,2,256,2,384]{2,1,0,4,3:T(2,128)(2,1)} %copy.35) | data formatting | bytes 6291456 | tf_op jit(solution)/shard_map/reshape | solution.py:281
  110.5 1.9 pad_maximum_fusion.1.feats
  112.5 208.5 %shard_map.93 = (bf16[8,192,512]{2,1,0:T(8,128)(2,1)}, bf16[8,192,512]{2,1,0:T(8,128)(2,1)}, f32[1536,256]{1,0:T(8,128)}) custom-call(bf16[2,2,192,2048]{3,2,1,0:T(8,128)(2,1)} %pad_maximum_fusion.1.feats, bf16[3072,4096]{1,0:T(8,128)(2,1)} %w_gate.1, bf16[3072,4096]{1,0:T(8,128)(2,1)} %w_up.1, bf16[256,1024]{1,0:T(8,128)(2,1)} %get-tuple-element.63.refs_0_, ...), custom_call_target="tpu_custom_call" | custom-call | flops 25999998976 | bytes 60000000 | tf_op jit(solution)/shard_map/pallas_call | solution.py:293
  321.0 2.1 select_bitcast_fusion
  323.1 1.3 copy.38
  324.4 1.3 copy.39
  326.4 1.8 convolution_convert_fusion.1
  (42 shorter events, 5.7 us)
Async XLA Ops:
  0.6 1.5 copy-start
  0.6 5.1 %copy-start.4 = (s32[512,2]{0,1:T(2,128)S(1)}, s32[512,2]{0,1:T(2,128)}, u32[]{:S(2)}) copy-start(s32[512,2]{0,1:T(2,128)} %param.10) | copy-start | bytes 12292
  0.7 5.1 %copy-start.5 = (s32[512,2]{0,1:T(2,128)S(1)}, s32[512,2]{0,1:T(2,128)}, u32[]{:S(2)}) copy-start(s32[512,2]{0,1:T(2,128)} %param.11) | copy-start | bytes 12292
  2.7 20.7 %collective-permute-start = (bf16[256,1536]{1,0:T(8,128)(2,1)S(1)}, bf16[256,1536]{1,0:T(8,128)(2,1)}, u32[]{:S(2)}, u32[]{:S(2)}) collective-permute-start(bf16[256,1536]{1,0:T(8,128)(2,1)S(1)} %convolution_convert_fusion.2), channel_id=1, source_target_pairs={{0,1},{1,0},{2,3},{3,2},{4,5},{5,4},{6,7},{7,6},{8,9},{9,8},{10,11... | collective-permute-start | bytes 2359304 | tf_op jit(solution)/shard_map/ppermute | solution.py:212
  37.3 19.0 %collective-permute-start.1 = (bf16[256,2,2,384]{3,0,2,1:T(8,128)(2,1)}, bf16[256,2,2,384]{3,0,2,1:T(8,128)(2,1)}, u32[]{:S(2)}, u32[]{:S(2)}) collective-permute-start(bf16[256,2,2,384]{3,0,2,1:T(8,128)(2,1)} %bitcast.62), channel_id=1, source_target_pairs={{0,8},{2,10},{4,12},{6,14},{8,0},{10,2},{12,4},{14,6},{16,24},{18,... | collective-permute-start | bytes 2359304 | tf_op jit(solution)/shard_map/ppermute | solution.py:206
  39.4 5.1 %copy-start.6 = (f32[256,1024]{1,0:T(8,128)S(1)}, f32[256,1024]{1,0:T(8,128)}, u32[]{:S(2)}) copy-start(f32[256,1024]{1,0:T(8,128)} %fusion.8) | copy-start | bytes 3145732
  62.2 17.9 %collective-permute-start.2 = (bf16[2,256,2,384]{3,1,2,0:T(8,128)(2,1)S(1)}, bf16[2,256,2,384]{3,1,2,0:T(8,128)(2,1)S(1)}, u32[]{:S(2)}, u32[]{:S(2)}) collective-permute-start(bf16[2,256,2,384]{3,1,2,0:T(8,128)(2,1)S(1)} %get-tuple-element.50), channel_id=1, source_target_pairs={{0,4},{2,6},{4,0},{6,2},{8,12},{10,14},{12,8},{14,10},{16,20},{18,... | collective-permute-start | bytes 2359304 | tf_op jit(solution)/shard_map/ppermute | solution.py:206
  84.7 1.6 copy-start.2
  84.7 1.8 copy-start.7
  85.0 14.2 %collective-permute-start.3 = (bf16[4,256,2,384]{3,1,2,0:T(8,128)(2,1)S(1)}, bf16[4,256,2,384]{3,1,2,0:T(8,128)(2,1)S(1)}, u32[]{:S(2)}, u32[]{:S(2)}) collective-permute-start(bf16[4,256,2,384]{3,1,2,0:T(8,128)(2,1)S(1)} %get-tuple-element.48), channel_id=1, source_target_pairs={{0,2},{2,0},{4,6},{6,4},{8,10},{10,8},{12,14},{14,12},{16,18},{18,... | collective-permute-start | bytes 4718600 | tf_op jit(solution)/shard_map/ppermute | solution.py:206
  94.7 3.6 %collective-permute-start.4 = (f32[256]{0:T(256)S(1)}, f32[256]{0:T(256)S(1)}, u32[]{:S(2)}, u32[]{:S(2)}) collective-permute-start(f32[256]{0:T(256)S(1)} %add_add_fusion), channel_id=1, source_target_pairs={{0,1},{1,0},{2,3},{3,2},{4,5},{5,4},{6,7},{7,6},{8,9},{9,8},{10,11... | collective-permute-start | bytes 3080 | tf_op jit(solution)/shard_map/ppermute | solution.py:212
  324.4 2.0 copy-start.3
  325.7 2.4 copy-start.1
